TPU v7x, 32 devices: a whole 2x2x4 slice. The times are simulated.
32 devices in a mesh: pipe: 4 (over x, core), ulys: 8 (over z, y).
Axes of the slice: x: 2, y: 2, z: 4, core: 2. Of those that a mesh axis runs over, the one named last changes fastest.
Arguments:
- activations: bfloat16 [4, 256, 3072], P('pipe', 'ulys'), may hold values from -6 to 6
- patch_index: int32 [4], P('pipe'), may hold values from 0 to 11
- modulation: float32 [4, 3, 3072], P('pipe'), may hold values from -4 to 4
- qkv_weight: bfloat16 [4, 3072, 9216], P('pipe', None, 'ulys'), may hold values from -0.109375 to 0.109375
- out_weight: bfloat16 [4, 3072, 3072], P('pipe', 'ulys'), may hold values from -0.109375 to 0.109375
- stale_cache: bfloat16 [4, 8, 3072, 2, 384], P('pipe', 'ulys'), may hold values from -360 to 360
- id_cache: bfloat16 [4, 8, 6, 32, 2, 384], P('pipe', 'ulys'), may hold values from -360 to 360
- region_ids: int32 [4, 256], P('pipe', 'ulys'), may hold values from 0 to 6
- id_counts: int32 [4, 6], P('pipe'), may hold values from 1 to 32, as said below
Outputs:
- next_activations: bfloat16 [4, 256, 3072], P('pipe', 'ulys')
Inputs may be any that keep to these rules, and one draw needn't show every extreme that they name: `id_counts`: in every section some subject has exactly 32 live identity tokens.
All inputs are finite; a program needn't handle non-finite values.
Results may differ from a plain program's by a relative error of at most 0.0117.
The roundings to bfloat16 on the way count: a program that leaves them out, or rounds other values in their place, can miss the bound.
Values may be sent and summed in bfloat16 or wider, within the bound.
No kernel may reach another device: no remote copies, remote signals or barrier semaphores. Data moves between devices by JAX's collectives and lax.ppermute only.
A program may use at most 128 MiB of HBM per device.

v0:
```python
import jax
import jax.numpy as jnp
from jax import lax
from jax.sharding import PartitionSpec as P

HD = 128
HPD = 3
GROUPS = 8
SUBJ = 6


NEG_BIG = -1e30


def as_sent(x):
    return jax.tree.map(lambda a: a.astype(jnp.bfloat16) if a.dtype == jnp.float32 else a, x)


def from_partner(x, axis, apart):
    return lax.ppermute(x, axis, [(i, i ^ 1 << apart) for i in range(lax.axis_size(axis))])


def passed_along(x, axis, by):
    size = lax.axis_size(axis)
    return lax.ppermute(x, axis, [(i, (i + by) % size) for i in range(size)])


def order_pair(mine, other, rank, level, axis):
    upper = rank // 2**level % 2
    first = jnp.where(upper == 1, other, mine)
    second = jnp.where(upper == 1, mine, other)
    return jnp.concatenate([first, second], axis=axis)


def block_attend(queries, keys, values, mask, factor):
    scores = jnp.einsum("qhd,khd->qhk", queries, keys, preferred_element_type=jnp.float32) * factor
    if mask is None:
        peak = jnp.max(scores, axis=2)
        weights = jnp.exp(scores - peak[:, :, None])
    else:
        wide = mask[:, None, :]
        peak = jnp.max(jnp.where(wide, scores, NEG_BIG), axis=2)
        weights = jnp.where(wide, jnp.exp(jnp.where(wide, scores - peak[:, :, None], 0.0)), 0.0)
    total = jnp.sum(weights, axis=2)
    output = jnp.einsum(
        "qhk,khd->qhd", weights.astype(jnp.bfloat16), values, preferred_element_type=jnp.float32
    )
    return (peak, total, output)


def merge_parts(first, second):
    peak = jnp.maximum(first[0], second[0])
    weight_one = jnp.exp(first[0] - peak)
    weight_two = jnp.exp(second[0] - peak)
    total = first[1] * weight_one + second[1] * weight_two
    output = first[2] * weight_one[:, :, None, None] + second[2] * weight_two[:, :, None, None]
    return (peak, total, output)


def merge_both(first, second):
    return merge_parts(first[:3], second[:3]) + merge_parts(first[3:], second[3:])


def shards(
    activations,
    patch_index,
    modulation,
    qkv_weight,
    out_weight,
    stale_cache,
    id_cache,
    region_ids,
    id_counts,
):
    ksplit = lax.axis_size("ulys") // GROUPS
    nbits = ksplit.bit_length() - 1
    rank = lax.axis_index("ulys") % ksplit
    rows = activations[0]
    modul = modulation[0]
    lifted = rows.astype(jnp.float32)
    center = jnp.mean(lifted, axis=1, keepdims=True)
    spread = jnp.mean(jnp.square(lifted - center), axis=1, keepdims=True)
    normed = (lifted - center) * lax.rsqrt(spread + 1e-06)
    hidden = (normed * (1.0 + modul[1]) + modul[0]).astype(jnp.bfloat16)
    all_rows, all_regions = (
        lax.all_gather(hidden, "ulys", axis=0, tiled=True),
        lax.all_gather(region_ids[0].astype(jnp.bfloat16), "ulys", axis=0, tiled=True),
    )
    total_rows = all_rows.shape[0]
    weight = qkv_weight[0]
    block_dims = HD // ksplit
    pieces = jnp.dot(all_rows, weight, preferred_element_type=jnp.float32).astype(jnp.bfloat16)[
        :, None, :
    ]
    for level in range(nbits):
        partner = from_partner(as_sent(pieces), "ulys", level).astype(pieces.dtype)
        pieces = order_pair(pieces, partner, rank, level, 1)
    fields = (
        pieces.reshape(total_rows, ksplit, 3, HPD, block_dims)
        .transpose(2, 0, 3, 1, 4)
        .reshape(3, total_rows, HPD, HD)
    )
    queries = fields[0]
    stored = stale_cache[0, 0]
    span = stored.shape[0]
    old_keys = stored[:, 0].reshape(span, HPD, HD)
    old_values = stored[:, 1].reshape(span, HPD, HD)
    patch = patch_index[0]
    per_block = span // total_rows
    owner = patch // per_block
    offset = patch % per_block * total_rows
    keys = jnp.where(
        rank == owner, lax.dynamic_update_slice(old_keys, fields[1], (offset, 0, 0)), old_keys
    )
    values = jnp.where(
        rank == owner, lax.dynamic_update_slice(old_values, fields[2], (offset, 0, 0)), old_values
    )
    factor = HD ** (-0.5)
    query_block = min(512, total_rows)
    block_count = total_rows // query_block

    def attend_rows(query_rows):
        return block_attend(query_rows, keys, values, None, factor)

    peaks, totals, outputs = lax.map(
        attend_rows, queries.reshape(block_count, query_block, HPD, HD)
    )
    peaks = peaks.reshape(total_rows, HPD)
    totals = totals.reshape(total_rows, HPD)
    outputs = outputs.reshape(total_rows, HPD, ksplit, block_dims)
    guests = id_cache[0, 0]
    id_slots = guests.shape[1]
    guest_keys = guests[:, :, 0].reshape(SUBJ * id_slots, HPD, HD)
    guest_values = guests[:, :, 1].reshape(SUBJ * id_slots, HPD, HD)
    slot_index = jnp.arange(id_slots, dtype=jnp.int32) + rank * id_slots
    valid = slot_index[None, :] < id_counts[0][:, None]
    subject = jnp.arange(1, SUBJ + 1).astype(jnp.bfloat16)
    match = all_regions[:, None] == subject[None, :]
    mask = (match[:, :, None] & valid[None]).reshape(total_rows, SUBJ * id_slots)
    guest_peak, guest_total, guest_out = block_attend(
        queries, guest_keys, guest_values, mask, factor
    )
    guest_out = guest_out.reshape(total_rows, HPD, ksplit, block_dims)
    state = (peaks, totals, outputs, guest_peak, guest_total, guest_out)
    for level in range(nbits):
        partner = from_partner(state, "ulys", level)
        state = merge_both(state, partner)
    own_out = lax.dynamic_index_in_dim(state[2], rank, 2, keepdims=False)
    guest_final = lax.dynamic_index_in_dim(state[5], rank, 2, keepdims=False)
    own_final = own_out / state[1][:, :, None]
    guest_final = guest_final / jnp.maximum(state[4], 1.0)[:, :, None]
    mixed = (own_final + guest_final).astype(jnp.bfloat16).reshape(total_rows, HPD * block_dims)
    proj_weight = out_weight[0]
    added = lax.psum_scatter(
        jnp.dot(mixed, proj_weight, preferred_element_type=jnp.float32).astype(jnp.bfloat16),
        "ulys",
        scatter_dimension=0,
        tiled=True,
    ).astype(jnp.float32)
    result = (lifted + modul[2] * added).astype(jnp.bfloat16)
    return passed_along(result[None], "pipe", 1)


def solution(mesh):
    placed = (
        P("pipe", "ulys", None),
        P("pipe"),
        P("pipe", None, None),
        P("pipe", None, "ulys"),
        P("pipe", "ulys", None),
        P("pipe", "ulys", None, None, None),
        P("pipe", "ulys", None, None, None, None),
        P("pipe", "ulys"),
        P("pipe", None),
    )
    return jax.shard_map(
        shards, mesh=mesh, in_specs=placed, out_specs=P("pipe", "ulys", None), check_vma=False
    )
```

profile of v0, /device:TPU:0, one launch (start us, length us, event | category | flops | bytes accessed | tf_op | source)
XLA Modules:
  0.0 155.9 jit_solution(1780168167759137213)
XLA Ops:
  6.5 0.0 copy-start
  6.5 0.0 all-gather.3.cloned.1.call-start
  6.5 0.9 fusion.58
  7.4 1.1 convert_reduce_fusion
  8.5 1.2 fusion.33
  9.7 1.7 %fusion.36 = bf16[32,3072]{1,0:T(8,128)(2,1)} fusion(bf16[1,32,3072]{2,1,0:T(8,128)(2,1)} %param.9, f32[3072]{0:T(1024)S(1)} %bitcast.108, f32[3072]{0:T(1024)S(1)} %bitcast.109, f32[32]{0:T(128)S(1)} %add_rsqrt_fusion, f32[32]{0:T(128)S(1)} %broadcast_multiply_fusion), kind=kLoop, calls=%fused_computation.37 | loop fusion | flops 589824 | bytes 418048 | tf_op jit(solution)/shard_map/convert_element_type | solution.py:84
  11.4 0.0 all-gather.3.cloned.1.call-update
  11.5 0.0 reduce-scatter.2.cloned.1.call-start
  12.2 12.4 %copy.13 = bf16[1,1,3072,2,384]{2,4,3,1,0:T(8,128)(2,1)} copy(bf16[1,1,3072,2,384]{4,3,2,1,0:T(2,128)(2,1)} %param.14) | data formatting | bytes 9437184 | tf_op args[5]
  24.6 0.0 copy-start.5
  24.6 2.7 %fusion.57 = (bf16[3072,1,384]{0,2,1:T(8,128)(2,1)S(1)}, bf16[3072,1,384]{0,2,1:T(8,128)(2,1)S(1)}) fusion(bf16[3072,2,384]{0,2,1:T(8,128)(2,1)} %bitcast.97), kind=kLoop, calls=%fused_computation.71 | loop fusion | bytes 9437184 | tf_op jit(solution)/shard_map/slice | solution.py:106
  27.3 0.0 copy-start.1
  27.3 0.0 copy-start.3
  27.4 0.0 copy-start.9
  27.4 0.0 copy-start.11
  27.4 0.0 copy-start.10
  27.4 1.4 copy-done.1
  28.8 0.1 constant_dynamic-slice_fusion
  28.8 0.7 copy-done.3
  29.5 0.8 copy.27
  30.3 0.8 copy.26
  31.1 0.0 copy-done.5
  31.1 1.5 slice_reduce_fusion
  32.6 0.7 reshape_squeeze.14
  33.3 0.1 lt.40
  33.4 0.0 copy-done.9
  33.4 0.1 broadcast_reduce_fusion
  33.5 0.1 lt.42
  33.6 0.7 reshape_squeeze.15
  34.3 0.0 copy-done.11
  34.3 0.6 dynamic-slice.8
  35.5 0.0 copy-done.10
  35.6 0.2 dynamic-update-slice.2
  35.8 23.7 %all-reduce = bf16[256]{0:T(256)(128)(2,1)S(1)} all-reduce(bf16[256]{0:T(256)(128)(2,1)S(1)} %dynamic-update-slice.2), channel_id=2, replica_groups=mesh['pipe'=4,'ulys'=8] {'ulys'}, use_global_device_ids=true, to_apply=%add | all-reduce | flops 256 | bytes 1024
  59.5 0.1 broadcast_compare_fusion
  59.6 0.7 bitcast_and_fusion
  60.3 5.7 %fusion.10 = bf16[256,1152]{1,0:T(8,128)(2,1)S(1)} fusion(bf16[256,3072]{1,0:T(8,128)(2,1)} %all-gather.3.cloned.1.call-done, bf16[1,3072,1152]{2,1,0:T(8,128)(2,1)} %param.12), kind=kOutput, calls=%fused_computation.12 | convolution fusion | flops 1812234240 | bytes 9240576 | tf_op jit(solution)/shard_map/dot_general | solution.py:92
  66.0 0.2 copy.14
  66.2 0.3 copy.15
  66.5 0.1 fusion.42
  66.6 0.1 copy.17
  66.7 0.7 constant_dynamic-update-slice_fusion.1
  67.5 0.1 copy.19
  67.6 0.7 constant_dynamic-update-slice_fusion
  68.3 3.2 %bitcast_reduce_fusion = (f32[256,3]{0,1:T(4,128)S(1)}, f32[3,3072,256]{2,1,0:T(8,128)S(1)}) fusion(bf16[3072,3,128]{0,2,1:T(8,128)(2,1)} %constant_dynamic-update-slice_fusion, bf16[3,256,3,1,128]{4,1,2,3,0:T(8,128)(2,1)S(1)} %bitcast.101), kind=kOutput, calls=%fused_computation.2 | convolution fusion | flops 608697600 | bytes 11996160 | tf_op jit(solution)/shard_map/while/body/eval_jaxpr/qhd,khd->qhk/dot_general | solution.py:36
  71.5 0.0 copy-done.6
  71.5 0.2 fusion.18
  71.8 0.0 copy-done.8
  71.8 0.2 fusion.59
  72.0 1.5 fusion.2
  73.6 0.1 copy-done.4
  73.7 2.4 %fusion.25 = f32[256,3,128]{0,2,1:T(8,128)} fusion(bf16[3072,3,128]{0,2,1:T(8,128)(2,1)S(1)} %copy-done.4, f32[3,3072,256]{2,1,0:T(8,128)S(1)} %get-tuple-element.33, f32[256,3]{0,1:T(4,128)S(1)} %get-tuple-element.32, f32[256,3]{0,1:T(4,128)S(1)} %fusion.2), kind=kOutput, calls=%fused_computation.25 | convolution fusion | flops 611155968 | bytes 12195840 | tf_op jit(solution)/shard_map/while/body/eval_jaxpr/qhk,khd->qhd/dot_general | solution.py:45
  76.1 0.0 copy-done.7
  76.1 1.4 fusion.24
  77.6 0.0 copy-done
  77.6 0.0 copy-start.2
  77.6 2.2 %convolution_convert_fusion = bf16[256,3072]{1,0:T(8,128)(2,1)} fusion(bf16[256,384]{0,1:T(8,128)(2,1)S(1)} %bitcast.107, bf16[1,384,3072]{2,1,0:T(8,128)(2,1)S(1)} %copy-done), kind=kOutput, calls=%fused_computation.11 | convolution fusion | flops 604766208 | bytes 4128768 | tf_op jit(solution)/shard_map/dot_general | solution.py:155
  79.7 0.0 reduce-scatter.2.cloned.1.call-update
  79.8 62.5 %reduce-scatter.2.cloned.1.call-done = bf16[32,3072]{1,0:T(8,128)(2,1)} async-done(((bf16[256,3072]{1,0:T(8,128)(2,1)}), bf16[32,3072]{1,0:T(8,128)(2,1)}) %reduce-scatter.2.cloned.1.call-update) | async-done | bytes 196624 | tf_op jit(solution)/shard_map/reduce_scatter | solution.py:154
  142.2 0.0 copy-done.2
  142.2 1.0 fusion.41
  143.2 0.1 collective-permute-start
  143.3 5.1 %collective-permute-done = bf16[1,32,3072]{2,1,0:T(8,128)(2,1)S(1)} collective-permute-done((bf16[1,32,3072]{2,1,0:T(8,128)(2,1)S(1)}, bf16[1,32,3072]{2,1,0:T(8,128)(2,1)S(1)}, u32[]{:S(2)}, u32[]{:S(2)}) %collective-permute-start) | collective-permute-done | bytes 196640 | tf_op jit(solution)/shard_map/ppermute | solution.py:25
  148.4 0.7 copy.37
  (13 shorter events, 0.1 us)
Async XLA Ops:
  6.5 71.0 %copy-start = (bf16[1,384,3072]{2,1,0:T(8,128)(2,1)S(1)}, bf16[1,384,3072]{2,1,0:T(8,128)(2,1)}, u32[]{:S(2)}) copy-start(bf16[1,384,3072]{2,1,0:T(8,128)(2,1)} %param.13) | copy-start | bytes 7077892
  6.5 53.7 %all-gather.3.cloned.1.call-start = ((), (), s32[]{:S(2)}) async-start(), calls=%async_computation.1 | async-start | bytes 1769472 | tf_op jit(solution)/shard_map/all_gather | solution.py:86
  11.5 130.8 %reduce-scatter.2.cloned.1.call-start = ((), (), s32[]{:S(2)}) async-start(), calls=%async_computation.2 | async-start | bytes 1769472 | tf_op jit(solution)/shard_map/reduce_scatter | solution.py:154
  24.6 6.5 %copy-start.5 = (bf16[1,1,6,32,2,384]{5,4,3,2,1,0:T(2,128)(2,1)S(1)}, bf16[1,1,6,32,2,384]{5,4,3,2,1,0:T(2,128)(2,1)}, u32[]{:S(2)}) copy-start(bf16[1,1,6,32,2,384]{5,4,3,2,1,0:T(2,128)(2,1)} %param.15) | copy-start | bytes 884740
  27.3 1.4 copy-start.1
  27.3 2.1 %copy-start.3 = (bf16[3072,1,384]{0,2,1:T(8,128)(2,1)}, bf16[3072,1,384]{0,2,1:T(8,128)(2,1)S(1)}, u32[]{:S(2)}) copy-start(bf16[3072,1,384]{0,2,1:T(8,128)(2,1)S(1)} %get-tuple-element.24) | copy-start | bytes 7077892
  27.4 6.0 %copy-start.9 = (s32[1,6]{1,0:T(1,128)S(1)}, s32[1,6]{1,0:T(1,128)}, u32[]{:S(2)}) copy-start(s32[1,6]{1,0:T(1,128)} %param.17) | copy-start | bytes 76
  27.4 6.9 %copy-start.11 = (u32[32]{0:T(128)S(1)}, u32[32]{0:T(128)}, u32[]{:S(2)}) copy-start(u32[32]{0:T(128)} %constant.94) | copy-start | bytes 388
  27.4 8.1 %copy-start.10 = (s32[1,32]{1,0:T(1,128)S(1)}, s32[1,32]{1,0:T(1,128)}, u32[]{:S(2)}) copy-start(s32[1,32]{1,0:T(1,128)} %param.16) | copy-start | bytes 388
  68.3 3.2 %copy-start.6 = (bf16[192,3,128]{2,1,0:T(4,128)(2,1)S(1)}, bf16[192,3,128]{2,1,0:T(4,128)(2,1)}, u32[]{:S(2)}) copy-start(bf16[192,3,128]{2,1,0:T(4,128)(2,1)} %reshape_squeeze.14) | copy-start | bytes 442372
  68.3 3.4 %copy-start.8 = (pred[256,192]{0,1:T(8,128)(4,1)S(1)}, pred[256,192]{0,1:T(8,128)(4,1)}, u32[]{:S(2)}) copy-start(pred[256,192]{0,1:T(8,128)(4,1)} %bitcast_and_fusion) | copy-start | bytes 147460
  72.0 1.7 %copy-start.4 = (bf16[3072,3,128]{0,2,1:T(8,128)(2,1)S(1)}, bf16[3072,3,128]{0,2,1:T(8,128)(2,1)}, u32[]{:S(2)}) copy-start(bf16[3072,3,128]{0,2,1:T(8,128)(2,1)} %constant_dynamic-update-slice_fusion.1) | copy-start | bytes 7077892
  73.7 2.4 %copy-start.7 = (bf16[192,3,128]{2,1,0:T(4,128)(2,1)S(1)}, bf16[192,3,128]{2,1,0:T(4,128)(2,1)}, u32[]{:S(2)}) copy-start(bf16[192,3,128]{2,1,0:T(4,128)(2,1)} %reshape_squeeze.15) | copy-start | bytes 442372
  77.6 64.7 %copy-start.2 = (bf16[1,32,3072]{2,1,0:T(8,128)(2,1)S(1)}, bf16[1,32,3072]{2,1,0:T(8,128)(2,1)}, u32[]{:S(2)}) copy-start(bf16[1,32,3072]{2,1,0:T(8,128)(2,1)} %param.9) | copy-start | bytes 589828
  143.2 5.1 %collective-permute-start = (bf16[1,32,3072]{2,1,0:T(8,128)(2,1)S(1)}, bf16[1,32,3072]{2,1,0:T(8,128)(2,1)S(1)}, u32[]{:S(2)}, u32[]{:S(2)}) collective-permute-start(bf16[1,32,3072]{2,1,0:T(8,128)(2,1)S(1)} %fusion.41), channel_id=1, source_target_pairs={{0,8},{8,16},{16,24},{24,0},{1,9},{9,17},{17,25},{25,1},{2,10},{10... | collective-permute-start | bytes 589832 | tf_op jit(solution)/shard_map/ppermute | solution.py:25
Sparse Core Ops, SparseCore 0:
  11.6 47.2 all-gather.2
  79.9 62.2 reduce-scatter.1
where the time goes:
time: 157 us; the launch traced here: 156 us
  waiting for transfers between devices  67.6 us (43%)
  local copies, waits for them, and re-layouts  26 us (17%)
  blocking collectives  23.7 us (15%)
  matrix products  15.1 us (10%)
  between operations  14.9 us (9%)
  other arithmetic  8.52 us (5%)
    reduce_scatter x1, waiting for transfers between devices, shards(): lax.psum_scatter(jnp.dot(mixed, proj_weight, preferred_element_type=jnp.f...  62.5 us
    unnamed x1, blocking collectives  23.7 us
    unnamed x31, local copies, waits for them, and re-layouts  17.8 us
    dot_general x1, matrix products, shards(): jnp.dot(all_rows, weight, preferred_element_type=jnp.float32)  5.69 us
    ppermute x1, waiting for transfers between devices, passed_along(): return lax.ppermute(x, axis, [(i, (i + by) % size) for i in range(size)])  5.08 us
    dot_general x2, matrix products, block_attend(): jnp.einsum('qhk,khd->qhd', weights.astype(jnp.bfloat16), values, preferre...  3.85 us
    dot_general x2, matrix products, block_attend(): jnp.einsum('qhd,khd->qhk', queries, keys, preferred_element_type=jnp.floa...  3.39 us
  transfers between devices with their start and end apart: 3, of which 2 were waited for; matrix products, arithmetic and copies ran while one was open for 14% of the time, Pallas kernels for 0%

commit v1 on v0

--- a/solution.py
+++ b/solution.py
@@ -1,6 +1,11 @@
+import functools
+import math
+
 import jax
 import jax.numpy as jnp
 from jax import lax
+from jax.experimental import pallas as pl
+from jax.experimental.pallas import tpu as pltpu
 from jax.sharding import PartitionSpec as P
 
 HD = 128
@@ -61,7 +66,7 @@
     return merge_parts(first[:3], second[:3]) + merge_parts(first[3:], second[3:])
 
 
-def shards(
+def shards_split(
     activations,
     patch_index,
     modulation,
@@ -161,6 +166,339 @@
     return passed_along(result[None], "pipe", 1)
 
 
+LANES = 128
+MIB = 1 << 20
+VMEM = pl.BlockSpec(memory_space=pltpu.VMEM)
+SMEM = pl.BlockSpec(memory_space=pltpu.SMEM)
+HBM = pl.BlockSpec(memory_space=pltpu.HBM)
+
+
+def in_hbm(x):
+    return pltpu.with_memory_space_constraint(x, pltpu.HBM)
+
+
+def limit(mib):
+    return pltpu.CompilerParams(vmem_limit_bytes=mib * MIB)
+
+
+def modulate_kernel(rows_ref, modul_ref, region_ref, block_ref, rows, modul, regions, sems):
+    tokens, width = rows.shape
+    copies = [
+        pltpu.make_async_copy(source, target, sems.at[i])
+        for i, (source, target) in enumerate(((rows_ref, rows), (modul_ref, modul), (region_ref, regions)))
+    ]
+    for copy in copies:
+        copy.start()
+    for copy in copies:
+        copy.wait()
+    lifted = rows[...].astype(jnp.float32)
+    center = jnp.mean(lifted, axis=1, keepdims=True)
+    spread = jnp.mean(jnp.square(lifted - center), axis=1, keepdims=True)
+    normed = (lifted - center) * lax.rsqrt(spread + 1e-06)
+    hidden = normed * (1.0 + modul[1]) + modul[0]
+    block_ref[:, :width] = hidden.astype(jnp.bfloat16)
+    square = (tokens, tokens)
+    diagonal = lax.broadcasted_iota(jnp.int32, square, 0) == lax.broadcasted_iota(jnp.int32, square, 1)
+    region = jnp.broadcast_to(regions[...].astype(jnp.float32), square)
+    column = jnp.sum(jnp.where(diagonal, region, 0.0), axis=1, keepdims=True)
+    block_ref[:, width:] = jnp.broadcast_to(column, (tokens, LANES)).astype(jnp.bfloat16)
+
+
+def modulate(rows, modul, region):
+    tokens, width = rows.shape
+    return pl.pallas_call(
+        modulate_kernel,
+        out_shape=jax.ShapeDtypeStruct((tokens, width + LANES), jnp.bfloat16),
+        in_specs=[HBM] * 3,
+        out_specs=VMEM,
+        scratch_shapes=[
+            pltpu.VMEM(rows.shape, rows.dtype),
+            pltpu.VMEM(modul.shape, modul.dtype),
+            pltpu.VMEM(region.shape, region.dtype),
+            pltpu.SemaphoreType.DMA((3,)),
+        ],
+        compiler_params=limit(8),
+        name="modulate",
+    )(*map(in_hbm, (rows, modul, region)))
+
+
+def stage_kernel(head, chunk, cache_ref, guest_ref, weight_ref, proj_ref, *refs):
+    keys_ref, values_ref, weight_out, proj_out, held, wide, sems = refs
+    span, slots = cache_ref.shape[0], guest_ref.shape[0]
+    lanes = pl.ds(head * HD, HD)
+    spans = [(at, chunk, cache_ref.at[pl.ds(at, chunk), :, lanes]) for at in range(0, span, chunk)]
+    spans.append((span, slots, guest_ref.at[:, :, lanes]))
+    copies = [
+        pltpu.make_async_copy(source, held.at[pl.ds(at, count)], sems.at[i])
+        for i, (at, count, source) in enumerate(spans)
+    ]
+    columns = pl.ds(head * weight_out.shape[1], weight_out.shape[1])
+    copies.append(pltpu.make_async_copy(weight_ref.at[:, columns], weight_out, sems.at[len(spans)]))
+    rows = pl.ds(head * HD, HD)
+    copies.append(pltpu.make_async_copy(proj_ref.at[rows], proj_out, sems.at[len(spans) + 1]))
+    for copy in copies:
+        copy.start()
+    pairs = held.reshape(2 * held.shape[0], HD)
+    for (first, count, _), copy in zip(spans, copies):
+        copy.wait()
+        for at in range(first, first + count, LANES):
+            step = min(LANES, first + count - at)
+            slot = wide.at[at // LANES % wide.shape[0]]
+            slot[pl.ds(0, 2 * step), :] = pairs[pl.ds(2 * at, 2 * step), :].astype(jnp.float32)
+            keys_ref[:, pl.ds(at, step)] = slot[pl.ds(0, step, stride=2), :].T.astype(jnp.bfloat16)
+            values_ref[pl.ds(at, step), :] = slot[pl.ds(1, step, stride=2), :].astype(jnp.bfloat16)
+    for copy in copies[len(spans) :]:
+        copy.wait()
+
+
+def stage(head, cache, guests, weight, proj):
+    span, slots = cache.shape[0], guests.shape[0]
+    total = span + slots
+    pieces = 4
+    shapes = [(HD, total), (total, HD), (weight.shape[0], HPD * HD), (HD, proj.shape[1])]
+    moved = 2 * (3 * total * HD + weight.size // 3 + proj.size // 3)
+    return pl.pallas_call(
+        functools.partial(stage_kernel, head, span // pieces),
+        out_shape=[jax.ShapeDtypeStruct(shape, jnp.bfloat16) for shape in shapes],
+        in_specs=[HBM] * 4,
+        out_specs=[VMEM] * 4,
+        scratch_shapes=[
+            pltpu.VMEM((total, 2, HD), jnp.bfloat16),
+            pltpu.VMEM((4, 2 * LANES, HD), jnp.float32),
+            pltpu.SemaphoreType.DMA((pieces + 3,)),
+        ],
+        compiler_params=limit(8),
+        cost_estimate=pl.CostEstimate(flops=0, bytes_accessed=moved, transcendentals=0),
+        name="stage",
+    )(*map(in_hbm, (cache, guests, weight, proj)))
+
+
+def project_kernel(parts, place, patch_ref, *refs):
+    blocks, weights, stored = refs[:parts], refs[parts : parts + 3], refs[parts + 3 : parts + 3 + 2 * HPD]
+    query_ref, region_ref, *fresh_refs = refs[parts + 3 + 2 * HPD : -1]
+    rows = refs[-1]
+    tokens = blocks[0].shape[0]
+    total = parts * tokens
+    width = weights[0].shape[0]
+    for r in range(parts):
+        rows[pl.ds(r * tokens, tokens)] = blocks[r][...]
+    region_ref[...] = rows[:, width:]
+    fresh = pl.ds(pl.multiple_of((2 * patch_ref[0] + place) * total, total), total)
+    for kind in range(3):
+        field = jnp.dot(rows[:, :width], weights[kind][...], preferred_element_type=jnp.float32)
+        field = field.astype(jnp.bfloat16)
+        if kind == 0:
+            query_ref[...] = field
+            continue
+        for h in range(HPD):
+            part = field[:, h * HD : (h + 1) * HD]
+            if kind == 1:
+                fresh_refs[2 * h][:, fresh] = part.T
+            else:
+                fresh_refs[2 * h + 1][fresh, :] = part
+
+
+def project(place, patch, blocks, weights, stored):
+    parts = len(blocks)
+    tokens, wide = blocks[0].shape
+    total = parts * tokens
+    out_shape = [
+        jax.ShapeDtypeStruct((total, HPD * HD), jnp.bfloat16),
+        jax.ShapeDtypeStruct((total, LANES), jnp.bfloat16),
+    ]
+    out_shape += [jax.ShapeDtypeStruct(array.shape, array.dtype) for array in stored]
+    first = 1 + parts + 3
+    return pl.pallas_call(
+        functools.partial(project_kernel, parts, place),
+        out_shape=out_shape,
+        in_specs=[SMEM] + [VMEM] * (parts + 3 + 2 * HPD),
+        out_specs=[VMEM] * len(out_shape),
+        scratch_shapes=[pltpu.VMEM((total, wide), jnp.bfloat16)],
+        input_output_aliases={first + i: 2 + i for i in range(2 * HPD)},
+        compiler_params=limit(8),
+        cost_estimate=pl.CostEstimate(
+            flops=2 * total * (wide - LANES) * 3 * HPD * HD, bytes_accessed=8 * MIB, transcendentals=0
+        ),
+        name="project",
+    )(patch, *blocks, *weights, *stored)
+
+
+def attend_kernel(order, outputs, counts_ref, modul_ref, *refs):
+    queries, regions, refs = refs[:2], refs[2:4], refs[4:]
+    stored, refs = refs[: 2 * HPD], refs[2 * HPD :]
+    projs, refs = refs[:HPD], refs[HPD:]
+    outs, refs = refs[: len(outputs)], refs[len(outputs) :]
+    scores, mixed = refs[:HPD], refs[HPD]
+    total, span = scores[0].shape
+    tokens = total // len(order)
+    width = projs[0].shape[1]
+    slots = stored[0].shape[1] - span
+    each = slots // SUBJ
+
+    def rows_of(arrays, columns):
+        half = arrays[0].shape[0] // tokens
+        return jnp.concatenate(
+            [arrays[r // half][pl.ds(r % half * tokens, tokens), columns] for r in order], axis=0
+        )
+
+    lane = lax.broadcasted_iota(jnp.int32, (1, slots), 1)
+    code = jnp.full((1, slots), -1.0, jnp.float32)
+    for s in range(SUBJ):
+        live = (lane >= s * each) & (lane < s * each + counts_ref[0, s])
+        code = jnp.where(live, s + 1.0, code)
+    match = code == rows_of(regions, pl.ds(0, LANES))[:, :1].astype(jnp.float32)
+    factor = HD ** (-0.5) * math.log2(math.e)
+    query = [rows_of(queries, pl.ds(h * HD, HD)) for h in range(HPD)]
+    chunk = 256
+    tops = [None] * HPD
+
+    def score(h, at):
+        found = jnp.dot(query[h], stored[2 * h][:, pl.ds(at, chunk)], preferred_element_type=jnp.float32)
+        scores[h][:, pl.ds(at, chunk)] = found
+        both = jnp.maximum(found[:, :LANES], found[:, LANES:])
+        tops[h] = both if tops[h] is None else jnp.maximum(tops[h], both)
+
+    for at in range(0, span, chunk):
+        score(0, at)
+    for h in range(HPD):
+        keys, values = stored[2 * h], stored[2 * h + 1]
+        peak = jnp.max(tops[h], axis=1, keepdims=True) * factor
+        found = jnp.dot(query[h], keys[:, span:], preferred_element_type=jnp.float32) * factor
+        sums = own = None
+        for at in range(0, span, chunk):
+            if h + 1 < HPD:
+                score(h + 1, at)
+            raised = jnp.exp2(scores[h][:, pl.ds(at, chunk)] * factor - peak)
+            both = raised[:, :LANES] + raised[:, LANES:]
+            product = jnp.dot(
+                raised.astype(jnp.bfloat16), values[pl.ds(at, chunk), :], preferred_element_type=jnp.float32
+            )
+            sums = both if sums is None else sums + both
+            own = product if own is None else own + product
+        own = own / jnp.sum(sums, axis=1, keepdims=True)
+        peak = jnp.max(jnp.where(match, found, NEG_BIG), axis=1, keepdims=True)
+        raised = jnp.where(match, jnp.exp2(jnp.where(match, found - peak, 0.0)), 0.0)
+        guest = jnp.dot(raised.astype(jnp.bfloat16), values[span:, :], preferred_element_type=jnp.float32)
+        guest = guest / jnp.maximum(jnp.sum(raised, axis=1, keepdims=True), 1.0)
+        mixed[:, pl.ds(h * HD, HD)] = (own + guest).astype(jnp.bfloat16)
+    for at in range(0, width, 512):
+        columns = pl.ds(at, 512)
+        proj = jnp.concatenate([share[:, columns] for share in projs], axis=0)
+        part = jnp.dot(mixed[...], proj, preferred_element_type=jnp.float32) * modul_ref[2, :, columns]
+        first = 0
+        for out, count in zip(outs, outputs):
+            terms = part[first : first + count * tokens]
+            out[pl.ds(0, terms.shape[0]), columns] = terms.astype(out.dtype)
+            first += count * tokens
+
+
+def attend(order, outputs, tokens, span, counts, modul, queries, regions, stored, projs):
+    total = len(order) * tokens
+    width = projs[0].shape[1]
+    return pl.pallas_call(
+        functools.partial(attend_kernel, order, [count for count, _ in outputs]),
+        out_shape=[jax.ShapeDtypeStruct((count * tokens, width), kind) for count, kind in outputs],
+        in_specs=[SMEM] + [VMEM] * (5 + 3 * HPD),
+        out_specs=[VMEM] * len(outputs),
+        scratch_shapes=[pltpu.VMEM((total, span), jnp.float32)] * HPD
+        + [pltpu.VMEM((total, HPD * HD), jnp.bfloat16)],
+        compiler_params=limit(16),
+        cost_estimate=pl.CostEstimate(
+            flops=2 * total * HPD * HD * (width + 2 * span),
+            bytes_accessed=16 * MIB,
+            transcendentals=HPD * total * span,
+        ),
+        name="attend",
+    )(counts, modul, *queries, *regions, *stored, *projs)
+
+
+def add_kernel(kept_ref, *refs):
+    total = kept_ref[...]
+    for came_ref in refs[:-1]:
+        total = total + came_ref[...].astype(jnp.float32)
+    refs[-1][...] = total.astype(jnp.bfloat16)
+
+
+def add_terms(kept, *came):
+    return pl.pallas_call(
+        add_kernel,
+        out_shape=jax.ShapeDtypeStruct(kept.shape, jnp.bfloat16),
+        in_specs=[VMEM] * (1 + len(came)),
+        out_specs=VMEM,
+        compiler_params=limit(4),
+        name="add_terms",
+    )(kept, *came)
+
+
+def shards_whole(
+    activations,
+    patch_index,
+    modulation,
+    qkv_weight,
+    out_weight,
+    stale_cache,
+    id_cache,
+    region_ids,
+    id_counts,
+):
+    pipes, group = lax.axis_size("pipe"), lax.axis_size("ulys")
+
+    def beside(x, apart):
+        return lax.ppermute(x, "ulys", [(i, i ^ apart) for i in range(group)])
+
+    def onward(x, apart):
+        pairs = [
+            (p * group + i, (p + 1) % pipes * group + (i ^ apart))
+            for p in range(pipes)
+            for i in range(group)
+        ]
+        return lax.ppermute(x, ("pipe", "ulys"), pairs)
+
+    hold = lax.optimization_barrier
+    rows = activations[0]
+    tokens = rows.shape[0]
+    modul = modulation.transpose(1, 0, 2)
+    stored = stale_cache[0, 0]
+    guests = id_cache[0, 0]
+    guests = guests.reshape(SUBJ * guests.shape[1], 2, HPD * HD)
+    staged = functools.partial(stage, cache=stored, guests=guests, weight=qkv_weight[0], proj=out_weight[0])
+    b0 = modulate(rows, modul, region_ids)
+    b4, b1, b3, b2 = (beside(b0, r) for r in (4, 1, 3, 2))
+    heads = [staged(h) for h in range(HPD)]
+    b4, *early = hold((b4, *heads[0], *heads[1]))
+    heads[0], heads[1] = early[: len(heads[0])], early[len(heads[0]) :]
+    b7, b5, b6 = beside(b4, 3), beside(b4, 1), beside(b4, 2)
+    weights, fields = [head[2] for head in heads], [array for head in heads for array in head[:2]]
+    query_near, region_near, *fields = project(0, patch_index, (b0, b1, b2, b3), weights, fields)
+    query_far, region_far, *fields = project(1, patch_index, (b4, b5, b6, b7), weights, fields)
+    attended = functools.partial(
+        attend,
+        tokens=tokens,
+        span=stored.shape[0],
+        counts=id_counts,
+        modul=modul,
+        regions=(region_near, region_far),
+        stored=fields,
+        projs=[head[3] for head in heads],
+    )
+    narrow, wide = (1, jnp.bfloat16), (1, jnp.float32)
+    t4, t7, t5, t6 = attended((4, 7, 5, 6), [wide] + [narrow] * 3, queries=(query_near, query_far))
+    t4, t7, t5, t6, query_near = hold((t4, t7, t5, t6, query_near))
+    t3, t1, t2, t0 = attended((3, 1, 2, 0), [narrow] * 4, queries=(query_near, query_far))
+    c7, c5, c6 = beside(t7, 3), beside(t5, 1), beside(t6, 2)
+    rows, t3, t1, t2, t0 = hold((rows, t3, t1, t2, t0))
+    before = onward(rows, 0)
+    c3, c1, c2 = onward(t3, 3), onward(t1, 1), onward(t2, 2)
+    s4 = add_terms(t4, c7, c5, c6)
+    s4, t0 = hold((s4, t0))
+    parts = before, c3, c1, c2, onward(s4, 4), onward(t0, 0)
+    return sum(part.astype(jnp.float32) for part in parts).astype(jnp.bfloat16)[None]
+
+
+def shards(*arrays):
+    return (shards_whole if lax.axis_size("ulys") == GROUPS else shards_split)(*arrays)
+
+
 def solution(mesh):
     placed = (
         P("pipe", "ulys", None),

time: 157 us -> 59 us (0.38)
  waiting for transfers between devices: 67.6 us -> 13.2 us
  local copies, waits for them, and re-layouts: 26 us -> 0.01 us
  starting transfers between devices: 0.1 us -> 24.4 us
  blocking collectives: 23.7 us -> 0 us
  Pallas kernels: 0 us -> 19.4 us
  matrix products: 15.1 us -> 0 us
  between operations: 14.9 us -> 0.76 us
  other arithmetic: 8.52 us -> 0.83 us
    reduce_scatter x1 -> x0, waiting for transfers between devices: 62.5 us -> none  [shards(): lax.psum_scatter(jnp.dot(mixed, proj_weight, preferred_element_type=jnp.f...]
    ppermute x1 -> x16, starting transfers between devices: 0.06 us -> 24.4 us  [the longest x10 15.3 us: beside(): return lax.ppermute(x, 'ulys', [(i, i ^ apart) for i in range(group)])]
    unnamed x1 -> x0, blocking collectives: 23.7 us -> none
    pallas_call x0 -> x9, Pallas kernels: none -> 19.4 us  [the longest x3 8.3 us: stage(): pl.pallas_call(functools.partial(stage_kernel, head, span // pieces), out...]
    unnamed x31 -> x6, local copies, waits for them, and re-layouts: 17.8 us -> 0.01 us
    dot_general x6 -> x0, matrix products: 15.1 us -> none  [the longest x1 5.69 us: shards(): jnp.dot(all_rows, weight, preferred_element_type=jnp.float32)]
    ppermute x1 -> x16, waiting for transfers between devices: 5.08 us -> 13.2 us  [the longest x10 6.76 us: beside(): return lax.ppermute(x, 'ulys', [(i, i ^ apart) for i in range(group)])]
    slice x2 -> x0, local copies, waits for them, and re-layouts: 4.2 us -> none  [the longest x1 2.74 us: shards(): old_keys = stored[:, 0].reshape(span, HPD, HD)]
  transfers between devices with their start and end apart: 3 -> 16, of which waited for: 2 -> 6; matrix products, arithmetic and copies ran while one was open for 14% -> 0% of each run, Pallas kernels for 0% -> 23%
where the time goes in v1:
time: 59 us; the launch traced here: 58.7 us
  starting transfers between devices  24.4 us (41%)
  Pallas kernels  19.4 us (33%)
  waiting for transfers between devices  13.2 us (22%)
  other arithmetic  0.83 us (1%)
  between operations  0.76 us (1%)
    ppermute x10, starting transfers between devices, beside(): return lax.ppermute(x, 'ulys', [(i, i ^ apart) for i in range(group)])  15.3 us
    ppermute x6, starting transfers between devices, onward(): return lax.ppermute(x, ('pipe', 'ulys'), pairs)  9.15 us
    pallas_call x3, Pallas kernels, stage(): pl.pallas_call(functools.partial(stage_kernel, head, span // pieces), out...  8.3 us
    pallas_call x2, Pallas kernels, attend(): pl.pallas_call(functools.partial(attend_kernel, order, [count for count,...  6.94 us
    ppermute x10, waiting for transfers between devices, beside(): return lax.ppermute(x, 'ulys', [(i, i ^ apart) for i in range(group)])  6.76 us
    ppermute x6, waiting for transfers between devices, onward(): return lax.ppermute(x, ('pipe', 'ulys'), pairs)  6.42 us
    pallas_call x2, Pallas kernels, project(): pl.pallas_call(functools.partial(project_kernel, parts, place), out_shape...  2.88 us
    pallas_call x1, Pallas kernels, modulate(): pl.pallas_call(modulate_kernel, out_shape=jax.ShapeDtypeStruct((tokens, w...  1.23 us
  transfers between devices with their start and end apart: 16, of which 6 were waited for; matrix products, arithmetic and copies ran while one was open for 0% of the time, Pallas kernels for 23%

profile of v1, /device:TPU:0, one launch (start us, length us, event | category | flops | bytes accessed | tf_op | source)
XLA Modules:
  0.0 58.7 jit_solution(6488145211610740061)
XLA Ops:
  0.0 1.2 %modulate.1.refs_0_ = bf16[32,3200]{1,0:T(8,128)(2,1)S(1)} custom-call(bf16[32,3072]{1,0:T(8,128)(2,1)} %bitcast.23, f32[3,1,3072]{2,1,0:T(1,128)} %bitcast.8, s32[1,32]{1,0:T(1,128)} %region_ref.1), custom_call_target="tpu_custom_call" | custom-call | tf_op jit(solution)/shard_map/modulate/pallas_call | solution.py:209
  1.2 4.1 %collective-permute-start.3 = (bf16[32,3200]{1,0:T(8,128)(2,1)S(1)}, bf16[32,3200]{1,0:T(8,128)(2,1)S(1)}, u32[]{:S(2)}, u32[]{:S(2)}) collective-permute-start(bf16[32,3200]{1,0:T(8,128)(2,1)S(1)} %modulate.1.refs_0_), channel_id=1, source_target_pairs={{0,4},{1,5},{2,6},{3,7},{4,0},{5,1},{6,2},{7,3},{8,12},{9,13},{10,... | collective-permute-start | bytes 614408 | tf_op jit(solution)/shard_map/ppermute | solution.py:447
  5.3 2.5 %collective-permute-start.2 = (bf16[32,3200]{1,0:T(8,128)(2,1)S(1)}, bf16[32,3200]{1,0:T(8,128)(2,1)S(1)}, u32[]{:S(2)}, u32[]{:S(2)}) collective-permute-start(bf16[32,3200]{1,0:T(8,128)(2,1)S(1)} %modulate.1.refs_0_), channel_id=1, source_target_pairs={{0,3},{1,2},{2,1},{3,0},{4,7},{5,6},{6,5},{7,4},{8,11},{9,10},{10,... | collective-permute-start | bytes 614408 | tf_op jit(solution)/shard_map/ppermute | solution.py:447
  7.9 0.4 collective-permute-start.1
  8.3 0.5 collective-permute-start
  8.8 2.8 %stage.4 = (bf16[128,3264]{1,0:T(8,128)(2,1)S(1)}, bf16[3264,128]{1,0:T(8,128)(2,1)S(1)}, bf16[3072,384]{1,0:T(8,128)(2,1)S(1)}, bf16[128,3072]{1,0:T(8,128)(2,1)S(1)}) custom-call(bf16[3072,2,384]{2,1,0:T(2,128)(2,1)} %bitcast.14, bf16[192,2,384]{2,1,0:T(2,128)(2,1)} %bitcast.20, bf16[3072,1152]{1,0:T(8,128)(2,1)} %bitcast.11, bf16[384,3072]{1,0:T(8,128)(2,1)} %bitcast.17), custom_call_target="tpu_custom_call" | custom-call | bytes 5652480 | tf_op jit(solution)/shard_map/stage/pallas_call | solution.py:260
  11.6 2.8 %stage.3 = (bf16[128,3264]{1,0:T(8,128)(2,1)S(1)}, bf16[3264,128]{1,0:T(8,128)(2,1)S(1)}, bf16[3072,384]{1,0:T(8,128)(2,1)S(1)}, bf16[128,3072]{1,0:T(8,128)(2,1)S(1)}) custom-call(bf16[3072,2,384]{2,1,0:T(2,128)(2,1)} %bitcast.15, bf16[192,2,384]{2,1,0:T(2,128)(2,1)} %bitcast.21, bf16[3072,1152]{1,0:T(8,128)(2,1)} %bitcast.12, bf16[384,3072]{1,0:T(8,128)(2,1)} %bitcast.18), custom_call_target="tpu_custom_call" | custom-call | bytes 5652480 | tf_op jit(solution)/shard_map/stage/pallas_call | solution.py:260
  14.4 0.5 collective-permute-done.3.refs_0_
  14.9 2.1 %collective-permute-start.6 = (bf16[32,3200]{1,0:T(8,128)(2,1)S(1)}, bf16[32,3200]{1,0:T(8,128)(2,1)S(1)}, u32[]{:S(2)}, u32[]{:S(2)}) collective-permute-start(bf16[32,3200]{1,0:T(8,128)(2,1)S(1)} %collective-permute-done.3.refs_0_), channel_id=1, source_target_pairs={{0,3},{1,2},{2,1},{3,0},{4,7},{5,6},{6,5},{7,4},{8,11},{9,10},{10,... | collective-permute-start | bytes 614408 | tf_op jit(solution)/shard_map/ppermute | solution.py:447
  17.0 0.9 %collective-permute-start.5 = (bf16[32,3200]{1,0:T(8,128)(2,1)S(1)}, bf16[32,3200]{1,0:T(8,128)(2,1)S(1)}, u32[]{:S(2)}, u32[]{:S(2)}) collective-permute-start(bf16[32,3200]{1,0:T(8,128)(2,1)S(1)} %collective-permute-done.3.refs_0_), channel_id=1, source_target_pairs={{0,2},{1,3},{2,0},{3,1},{4,6},{5,7},{6,4},{7,5},{8,10},{9,11},{10,... | collective-permute-start | bytes 614408 | tf_op jit(solution)/shard_map/ppermute | solution.py:447
  17.9 0.0 collective-permute-done.2.refs_3_
  17.9 1.1 %collective-permute-start.4 = (bf16[32,3200]{1,0:T(8,128)(2,1)S(1)}, bf16[32,3200]{1,0:T(8,128)(2,1)S(1)}, u32[]{:S(2)}, u32[]{:S(2)}) collective-permute-start(bf16[32,3200]{1,0:T(8,128)(2,1)S(1)} %collective-permute-done.3.refs_0_), channel_id=1, source_target_pairs={{0,1},{1,0},{2,3},{3,2},{4,5},{5,4},{6,7},{7,6},{8,9},{9,8},{10,11... | collective-permute-start | bytes 614408 | tf_op jit(solution)/shard_map/ppermute | solution.py:447
  19.0 2.8 %stage.5 = (bf16[128,3264]{1,0:T(8,128)(2,1)S(1)}, bf16[3264,128]{1,0:T(8,128)(2,1)S(1)}, bf16[3072,384]{1,0:T(8,128)(2,1)S(1)}, bf16[128,3072]{1,0:T(8,128)(2,1)S(1)}) custom-call(bf16[3072,2,384]{2,1,0:T(2,128)(2,1)} %bitcast.16, bf16[192,2,384]{2,1,0:T(2,128)(2,1)} %bitcast.22, bf16[3072,1152]{1,0:T(8,128)(2,1)} %bitcast.13, bf16[384,3072]{1,0:T(8,128)(2,1)} %bitcast.19), custom_call_target="tpu_custom_call" | custom-call | bytes 5652480 | tf_op jit(solution)/shard_map/stage/pallas_call | solution.py:260
  22.4 0.0 collective-permute-done.1.refs_2_
  22.4 0.0 collective-permute-done.refs_1_
  22.4 1.4 %project.2 = (bf16[128,384]{1,0:T(8,128)(2,1)S(1)}, bf16[128,128]{1,0:T(8,128)(2,1)S(1)}, bf16[128,3264]{1,0:T(8,128)(2,1)S(1)}, bf16[3264,128]{1,0:T(8,128)(2,1...) custom-call(s32[1]{0:T(128)S(6)} %copy.34.patch_ref, ...), custom_call_target="tpu_custom_call", output_to_operand_aliasing={{2}: (8, {}), {3}: (9, {}), {4}: (10, {}), {5}: (11, {}), {... | custom-call | flops 905969664 | bytes 8388608 | tf_op jit(solution)/shard_map/project/pallas_call | solution.py:311
  23.9 2.5 %collective-permute-done.6.refs_3_ = bf16[32,3200]{1,0:T(8,128)(2,1)S(1)} collective-permute-done((bf16[32,3200]{1,0:T(8,128)(2,1)S(1)}, bf16[32,3200]{1,0:T(8,128)(2,1)S(1)}, u32[]{:S(2)}, u32[]{:S(2)}) %collective-permute-start.6) | collective-permute-done | bytes 204832 | tf_op jit(solution)/shard_map/ppermute | solution.py:447
  26.3 2.9 %collective-permute-done.5.refs_2_ = bf16[32,3200]{1,0:T(8,128)(2,1)S(1)} collective-permute-done((bf16[32,3200]{1,0:T(8,128)(2,1)S(1)}, bf16[32,3200]{1,0:T(8,128)(2,1)S(1)}, u32[]{:S(2)}, u32[]{:S(2)}) %collective-permute-start.5) | collective-permute-done | bytes 204832 | tf_op jit(solution)/shard_map/ppermute | solution.py:447
  29.3 0.0 collective-permute-done.4.refs_1_
  29.3 0.0 copy-start
  29.3 0.0 copy-start.1
  29.3 1.4 %project.3 = (bf16[128,384]{1,0:T(8,128)(2,1)S(1)}, bf16[128,128]{1,0:T(8,128)(2,1)S(1)}, bf16[128,3264]{1,0:T(8,128)(2,1)S(1)}, bf16[3264,128]{1,0:T(8,128)(2,1...) custom-call(s32[1]{0:T(128)S(6)} %copy.34.patch_ref, ...), custom_call_target="tpu_custom_call", output_to_operand_aliasing={{2}: (8, {}), {3}: (9, {}), {4}: (10, {}), {5}: (11, {}), {... | custom-call | flops 905969664 | bytes 8388608 | tf_op jit(solution)/shard_map/project/pallas_call | solution.py:311
  30.7 0.0 copy-done
  30.7 0.0 copy-done.1
  30.8 3.5 %attend.2 = (f32[32,3072]{1,0:T(8,128)S(1)}, bf16[32,3072]{1,0:T(8,128)(2,1)S(1)}, bf16[32,3072]{1,0:T(8,128)(2,1)S(1)}, bf16[32,3072]{1,0:T(8,128)(2,1)S(1)}) custom-call(s32[1,6]{1,0:T(1,128)S(1)} %copy-done.1, f32[3,1,3072]{2,1,0:T(1,128)S(1)} %bitcast.9, bf16[128,384]{1,0:T(8,128)(2,1)S(1)} %get-tuple-element.103.refs_0_, ...), custom_call_target="tpu_custom_call" | custom-call | flops 905969664 | bytes 16777216 | tf_op jit(solution)/shard_map/attend/pallas_call | solution.py:398
  34.2 0.0 copy-start.2
  34.3 1.6 %collective-permute-start.11 = (bf16[32,3072]{1,0:T(8,128)(2,1)S(1)}, bf16[32,3072]{1,0:T(8,128)(2,1)S(1)}, u32[]{:S(2)}, u32[]{:S(2)}) collective-permute-start(bf16[32,3072]{1,0:T(8,128)(2,1)S(1)} %get-tuple-element.113), channel_id=1, source_target_pairs={{0,3},{1,2},{2,1},{3,0},{4,7},{5,6},{6,5},{7,4},{8,11},{9,10},{10,... | collective-permute-start | bytes 589832 | tf_op jit(solution)/shard_map/ppermute | solution.py:447
  35.8 0.5 collective-permute-start.12
  36.3 3.5 %attend.3 = (bf16[32,3072]{1,0:T(8,128)(2,1)S(1)}, bf16[32,3072]{1,0:T(8,128)(2,1)S(1)}, bf16[32,3072]{1,0:T(8,128)(2,1)S(1)}, bf16[32,3072]{1,0:T(8,128)(2,1)S(1)}) custom-call(s32[1,6]{1,0:T(1,128)S(1)} %copy-done.1, f32[3,1,3072]{2,1,0:T(1,128)S(1)} %bitcast.10, bf16[128,384]{1,0:T(8,128)(2,1)S(1)} %get-tuple-element.103.refs_0_, ...), custom_call_target="tpu_custom_call" | custom-call | flops 905969664 | bytes 16777216 | tf_op jit(solution)/shard_map/attend/pallas_call | solution.py:398
  39.8 1.5 %collective-permute-start.13 = (bf16[32,3072]{1,0:T(8,128)(2,1)S(1)}, bf16[32,3072]{1,0:T(8,128)(2,1)S(1)}, u32[]{:S(2)}, u32[]{:S(2)}) collective-permute-start(bf16[32,3072]{1,0:T(8,128)(2,1)S(1)} %get-tuple-element.115), channel_id=1, source_target_pairs={{0,2},{1,3},{2,0},{3,1},{4,6},{5,7},{6,4},{7,5},{8,10},{9,11},{10,... | collective-permute-start | bytes 589832 | tf_op jit(solution)/shard_map/ppermute | solution.py:447
  41.3 0.0 copy-done.2
  41.3 0.0 collective-permute-start.7
  41.4 2.7 %collective-permute-start.8 = (bf16[32,3072]{1,0:T(8,128)(2,1)S(1)}, bf16[32,3072]{1,0:T(8,128)(2,1)S(1)}, u32[]{:S(2)}, u32[]{:S(2)}) collective-permute-start(bf16[32,3072]{1,0:T(8,128)(2,1)S(1)} %get-tuple-element.109), channel_id=1, source_target_pairs={{0,11},{1,10},{2,9},{3,8},{4,15},{5,14},{6,13},{7,12},{8,19},{9,18... | collective-permute-start | bytes 589832 | tf_op jit(solution)/shard_map/ppermute | solution.py:455
  44.1 0.0 collective-permute-done.11.refs_0_
  44.1 0.0 collective-permute-start.9
  44.1 0.8 %collective-permute-done.12.refs_1_ = bf16[32,3072]{1,0:T(8,128)(2,1)S(1)} collective-permute-done((bf16[32,3072]{1,0:T(8,128)(2,1)S(1)}, bf16[32,3072]{1,0:T(8,128)(2,1)S(1)}, u32[]{:S(2)}, u32[]{:S(2)}) %collective-permute-start.12) | collective-permute-done | bytes 196640 | tf_op jit(solution)/shard_map/ppermute | solution.py:447
  44.9 0.9 %collective-permute-start.10 = (bf16[32,3072]{1,0:T(8,128)(2,1)S(1)}, bf16[32,3072]{1,0:T(8,128)(2,1)S(1)}, u32[]{:S(2)}, u32[]{:S(2)}) collective-permute-start(bf16[32,3072]{1,0:T(8,128)(2,1)S(1)} %get-tuple-element.111), channel_id=1, source_target_pairs={{0,10},{1,11},{2,8},{3,9},{4,14},{5,15},{6,12},{7,13},{8,18},{9,19... | collective-permute-start | bytes 589832 | tf_op jit(solution)/shard_map/ppermute | solution.py:455
  45.7 0.0 collective-permute-done.13.refs_2_
  45.8 0.1 add_terms.1
  45.9 2.9 %collective-permute-start.14 = (bf16[32,3072]{1,0:T(8,128)(2,1)S(1)}, bf16[32,3072]{1,0:T(8,128)(2,1)S(1)}, u32[]{:S(2)}, u32[]{:S(2)}) collective-permute-start(bf16[32,3072]{1,0:T(8,128)(2,1)S(1)} %add_terms.1), channel_id=1, source_target_pairs={{0,12},{1,13},{2,14},{3,15},{4,8},{5,9},{6,10},{7,11},{8,20},{9,21... | collective-permute-start | bytes 589832 | tf_op jit(solution)/shard_map/ppermute | solution.py:455
  48.7 0.0 collective-permute-done.7
  48.7 2.7 %collective-permute-start.15 = (bf16[32,3072]{1,0:T(8,128)(2,1)S(1)}, bf16[32,3072]{1,0:T(8,128)(2,1)S(1)}, u32[]{:S(2)}, u32[]{:S(2)}) collective-permute-start(bf16[32,3072]{1,0:T(8,128)(2,1)S(1)} %get-tuple-element.118), channel_id=1, source_target_pairs={{0,8},{1,9},{2,10},{3,11},{4,12},{5,13},{6,14},{7,15},{8,16},{9,17... | collective-permute-start | bytes 589832 | tf_op jit(solution)/shard_map/ppermute | solution.py:455
  51.4 0.0 collective-permute-done.8
  51.4 2.6 %collective-permute-done.9 = bf16[32,3072]{1,0:T(8,128)(2,1)S(1)} collective-permute-done((bf16[32,3072]{1,0:T(8,128)(2,1)S(1)}, bf16[32,3072]{1,0:T(8,128)(2,1)S(1)}, u32[]{:S(2)}, u32[]{:S(2)}) %collective-permute-start.9) | collective-permute-done | bytes 196640 | tf_op jit(solution)/shard_map/ppermute | solution.py:455
  54.1 3.8 %collective-permute-done.10 = bf16[32,3072]{1,0:T(8,128)(2,1)S(1)} collective-permute-done((bf16[32,3072]{1,0:T(8,128)(2,1)S(1)}, bf16[32,3072]{1,0:T(8,128)(2,1)S(1)}, u32[]{:S(2)}, u32[]{:S(2)}) %collective-permute-start.10) | collective-permute-done | bytes 196640 | tf_op jit(solution)/shard_map/ppermute | solution.py:455
  57.8 0.0 collective-permute-done.14
  57.8 0.0 collective-permute-done.15
  57.8 0.8 %fusion = bf16[1,32,3072]{2,1,0:T(8,128)(2,1)} fusion(bf16[32,3072]{1,0:T(8,128)(2,1)S(1)} %collective-permute-done.15, bf16[32,3072]{1,0:T(8,128)(2,1)S(1)} %collective-permute-done.14, bf16[32,3072]{1,0:T(8,128)(2,1)S(1)} %collective-permute-done.10, bf16[32,3072]{1,0:T(8,128)(2,1)S(1)} %collective-permute-done.9, ...), kind=kLoop, calls=%fused_computation.1 | loop fusion | flops 1179648 | bytes 1376256 | tf_op jit(solution)/shard_map/broadcast_in_dim | solution.py:495
Async XLA Ops:
  1.2 13.7 %collective-permute-start.3 = (bf16[32,3200]{1,0:T(8,128)(2,1)S(1)}, bf16[32,3200]{1,0:T(8,128)(2,1)S(1)}, u32[]{:S(2)}, u32[]{:S(2)}) collective-permute-start(bf16[32,3200]{1,0:T(8,128)(2,1)S(1)} %modulate.1.refs_0_), channel_id=1, source_target_pairs={{0,4},{1,5},{2,6},{3,7},{4,0},{5,1},{6,2},{7,3},{8,12},{9,13},{10,... | collective-permute-start | bytes 614408 | tf_op jit(solution)/shard_map/ppermute | solution.py:447
  5.3 12.6 %collective-permute-start.2 = (bf16[32,3200]{1,0:T(8,128)(2,1)S(1)}, bf16[32,3200]{1,0:T(8,128)(2,1)S(1)}, u32[]{:S(2)}, u32[]{:S(2)}) collective-permute-start(bf16[32,3200]{1,0:T(8,128)(2,1)S(1)} %modulate.1.refs_0_), channel_id=1, source_target_pairs={{0,3},{1,2},{2,1},{3,0},{4,7},{5,6},{6,5},{7,4},{8,11},{9,10},{10,... | collective-permute-start | bytes 614408 | tf_op jit(solution)/shard_map/ppermute | solution.py:447
  7.9 14.5 %collective-permute-start.1 = (bf16[32,3200]{1,0:T(8,128)(2,1)S(1)}, bf16[32,3200]{1,0:T(8,128)(2,1)S(1)}, u32[]{:S(2)}, u32[]{:S(2)}) collective-permute-start(bf16[32,3200]{1,0:T(8,128)(2,1)S(1)} %modulate.1.refs_0_), channel_id=1, source_target_pairs={{0,2},{1,3},{2,0},{3,1},{4,6},{5,7},{6,4},{7,5},{8,10},{9,11},{10,... | collective-permute-start | bytes 614408 | tf_op jit(solution)/shard_map/ppermute | solution.py:447
  8.3 14.1 %collective-permute-start = (bf16[32,3200]{1,0:T(8,128)(2,1)S(1)}, bf16[32,3200]{1,0:T(8,128)(2,1)S(1)}, u32[]{:S(2)}, u32[]{:S(2)}) collective-permute-start(bf16[32,3200]{1,0:T(8,128)(2,1)S(1)} %modulate.1.refs_0_), channel_id=1, source_target_pairs={{0,1},{1,0},{2,3},{3,2},{4,5},{5,4},{6,7},{7,6},{8,9},{9,8},{10,11... | collective-permute-start | bytes 614408 | tf_op jit(solution)/shard_map/ppermute | solution.py:447
  14.9 11.4 %collective-permute-start.6 = (bf16[32,3200]{1,0:T(8,128)(2,1)S(1)}, bf16[32,3200]{1,0:T(8,128)(2,1)S(1)}, u32[]{:S(2)}, u32[]{:S(2)}) collective-permute-start(bf16[32,3200]{1,0:T(8,128)(2,1)S(1)} %collective-permute-done.3.refs_0_), channel_id=1, source_target_pairs={{0,3},{1,2},{2,1},{3,0},{4,7},{5,6},{6,5},{7,4},{8,11},{9,10},{10,... | collective-permute-start | bytes 614408 | tf_op jit(solution)/shard_map/ppermute | solution.py:447
  17.0 12.3 %collective-permute-start.5 = (bf16[32,3200]{1,0:T(8,128)(2,1)S(1)}, bf16[32,3200]{1,0:T(8,128)(2,1)S(1)}, u32[]{:S(2)}, u32[]{:S(2)}) collective-permute-start(bf16[32,3200]{1,0:T(8,128)(2,1)S(1)} %collective-permute-done.3.refs_0_), channel_id=1, source_target_pairs={{0,2},{1,3},{2,0},{3,1},{4,6},{5,7},{6,4},{7,5},{8,10},{9,11},{10,... | collective-permute-start | bytes 614408 | tf_op jit(solution)/shard_map/ppermute | solution.py:447
  17.9 11.3 %collective-permute-start.4 = (bf16[32,3200]{1,0:T(8,128)(2,1)S(1)}, bf16[32,3200]{1,0:T(8,128)(2,1)S(1)}, u32[]{:S(2)}, u32[]{:S(2)}) collective-permute-start(bf16[32,3200]{1,0:T(8,128)(2,1)S(1)} %collective-permute-done.3.refs_0_), channel_id=1, source_target_pairs={{0,1},{1,0},{2,3},{3,2},{4,5},{5,4},{6,7},{7,6},{8,9},{9,8},{10,11... | collective-permute-start | bytes 614408 | tf_op jit(solution)/shard_map/ppermute | solution.py:447
  29.3 1.4 %copy-start = (f32[1,3,3072]{2,0,1:T(1,128)S(1)}, f32[1,3,3072]{2,0,1:T(1,128)}, u32[]{:S(2)}) copy-start(f32[1,3,3072]{2,0,1:T(1,128)} %param.11) | copy-start | bytes 110596
  29.3 1.5 %copy-start.1 = (s32[1,6]{1,0:T(1,128)S(1)}, s32[1,6]{1,0:T(1,128)}, u32[]{:S(2)}) copy-start(s32[1,6]{1,0:T(1,128)} %counts_ref.3) | copy-start | bytes 76
  34.2 7.1 %copy-start.2 = (bf16[1,32,3072]{2,1,0:T(8,128)(2,1)S(1)}, bf16[1,32,3072]{2,1,0:T(8,128)(2,1)}, u32[]{:S(2)}) copy-start(bf16[1,32,3072]{2,1,0:T(8,128)(2,1)} %param.9) | copy-start | bytes 589828
  34.3 9.8 %collective-permute-start.11 = (bf16[32,3072]{1,0:T(8,128)(2,1)S(1)}, bf16[32,3072]{1,0:T(8,128)(2,1)S(1)}, u32[]{:S(2)}, u32[]{:S(2)}) collective-permute-start(bf16[32,3072]{1,0:T(8,128)(2,1)S(1)} %get-tuple-element.113), channel_id=1, source_target_pairs={{0,3},{1,2},{2,1},{3,0},{4,7},{5,6},{6,5},{7,4},{8,11},{9,10},{10,... | collective-permute-start | bytes 589832 | tf_op jit(solution)/shard_map/ppermute | solution.py:447
  35.8 9.0 %collective-permute-start.12 = (bf16[32,3072]{1,0:T(8,128)(2,1)S(1)}, bf16[32,3072]{1,0:T(8,128)(2,1)S(1)}, u32[]{:S(2)}, u32[]{:S(2)}) collective-permute-start(bf16[32,3072]{1,0:T(8,128)(2,1)S(1)} %get-tuple-element.114), channel_id=1, source_target_pairs={{0,1},{1,0},{2,3},{3,2},{4,5},{5,4},{6,7},{7,6},{8,9},{9,8},{10,11... | collective-permute-start | bytes 589832 | tf_op jit(solution)/shard_map/ppermute | solution.py:447
  39.8 6.0 %collective-permute-start.13 = (bf16[32,3072]{1,0:T(8,128)(2,1)S(1)}, bf16[32,3072]{1,0:T(8,128)(2,1)S(1)}, u32[]{:S(2)}, u32[]{:S(2)}) collective-permute-start(bf16[32,3072]{1,0:T(8,128)(2,1)S(1)} %get-tuple-element.115), channel_id=1, source_target_pairs={{0,2},{1,3},{2,0},{3,1},{4,6},{5,7},{6,4},{7,5},{8,10},{9,11},{10,... | collective-permute-start | bytes 589832 | tf_op jit(solution)/shard_map/ppermute | solution.py:447
  41.3 7.4 %collective-permute-start.7 = (bf16[32,3072]{1,0:T(8,128)(2,1)S(1)}, bf16[32,3072]{1,0:T(8,128)(2,1)S(1)}, u32[]{:S(2)}, u32[]{:S(2)}) collective-permute-start(bf16[32,3072]{1,0:T(8,128)(2,1)S(1)} %bitcast.24), channel_id=1, source_target_pairs={{0,8},{1,9},{2,10},{3,11},{4,12},{5,13},{6,14},{7,15},{8,16},{9,17... | collective-permute-start | bytes 589832 | tf_op jit(solution)/shard_map/ppermute | solution.py:455
  41.4 10.1 %collective-permute-start.8 = (bf16[32,3072]{1,0:T(8,128)(2,1)S(1)}, bf16[32,3072]{1,0:T(8,128)(2,1)S(1)}, u32[]{:S(2)}, u32[]{:S(2)}) collective-permute-start(bf16[32,3072]{1,0:T(8,128)(2,1)S(1)} %get-tuple-element.109), channel_id=1, source_target_pairs={{0,11},{1,10},{2,9},{3,8},{4,15},{5,14},{6,13},{7,12},{8,19},{9,18... | collective-permute-start | bytes 589832 | tf_op jit(solution)/shard_map/ppermute | solution.py:455
  44.1 10.0 %collective-permute-start.9 = (bf16[32,3072]{1,0:T(8,128)(2,1)S(1)}, bf16[32,3072]{1,0:T(8,128)(2,1)S(1)}, u32[]{:S(2)}, u32[]{:S(2)}) collective-permute-start(bf16[32,3072]{1,0:T(8,128)(2,1)S(1)} %get-tuple-element.110), channel_id=1, source_target_pairs={{0,9},{1,8},{2,11},{3,10},{4,13},{5,12},{6,15},{7,14},{8,17},{9,16... | collective-permute-start | bytes 589832 | tf_op jit(solution)/shard_map/ppermute | solution.py:455
  44.9 13.0 %collective-permute-start.10 = (bf16[32,3072]{1,0:T(8,128)(2,1)S(1)}, bf16[32,3072]{1,0:T(8,128)(2,1)S(1)}, u32[]{:S(2)}, u32[]{:S(2)}) collective-permute-start(bf16[32,3072]{1,0:T(8,128)(2,1)S(1)} %get-tuple-element.111), channel_id=1, source_target_pairs={{0,10},{1,11},{2,8},{3,9},{4,14},{5,15},{6,12},{7,13},{8,18},{9,19... | collective-permute-start | bytes 589832 | tf_op jit(solution)/shard_map/ppermute | solution.py:455
  45.9 12.0 %collective-permute-start.14 = (bf16[32,3072]{1,0:T(8,128)(2,1)S(1)}, bf16[32,3072]{1,0:T(8,128)(2,1)S(1)}, u32[]{:S(2)}, u32[]{:S(2)}) collective-permute-start(bf16[32,3072]{1,0:T(8,128)(2,1)S(1)} %add_terms.1), channel_id=1, source_target_pairs={{0,12},{1,13},{2,14},{3,15},{4,8},{5,9},{6,10},{7,11},{8,20},{9,21... | collective-permute-start | bytes 589832 | tf_op jit(solution)/shard_map/ppermute | solution.py:455
  48.7 9.1 %collective-permute-start.15 = (bf16[32,3072]{1,0:T(8,128)(2,1)S(1)}, bf16[32,3072]{1,0:T(8,128)(2,1)S(1)}, u32[]{:S(2)}, u32[]{:S(2)}) collective-permute-start(bf16[32,3072]{1,0:T(8,128)(2,1)S(1)} %get-tuple-element.118), channel_id=1, source_target_pairs={{0,8},{1,9},{2,10},{3,11},{4,12},{5,13},{6,14},{7,15},{8,16},{9,17... | collective-permute-start | bytes 589832 | tf_op jit(solution)/shard_map/ppermute | solution.py:455

commit v2 on v1

--- a/solution.py
+++ b/solution.py
@@ -349,14 +349,17 @@
     match = code == rows_of(regions, pl.ds(0, LANES))[:, :1].astype(jnp.float32)
     factor = HD ** (-0.5) * math.log2(math.e)
     query = [rows_of(queries, pl.ds(h * HD, HD)) for h in range(HPD)]
-    chunk = 256
+    chunk = 512
     tops = [None] * HPD
+
+    def fold(join, found, whole):
+        parts = [found[:, i : i + LANES] for i in range(0, found.shape[1], LANES)]
+        return functools.reduce(join, parts if whole is None else [whole, *parts])
 
     def score(h, at):
         found = jnp.dot(query[h], stored[2 * h][:, pl.ds(at, chunk)], preferred_element_type=jnp.float32)
         scores[h][:, pl.ds(at, chunk)] = found
-        both = jnp.maximum(found[:, :LANES], found[:, LANES:])
-        tops[h] = both if tops[h] is None else jnp.maximum(tops[h], both)
+        tops[h] = fold(jnp.maximum, found, tops[h])
 
     for at in range(0, span, chunk):
         score(0, at)
@@ -369,11 +372,10 @@
             if h + 1 < HPD:
                 score(h + 1, at)
             raised = jnp.exp2(scores[h][:, pl.ds(at, chunk)] * factor - peak)
-            both = raised[:, :LANES] + raised[:, LANES:]
+            sums = fold(jnp.add, raised, sums)
             product = jnp.dot(
                 raised.astype(jnp.bfloat16), values[pl.ds(at, chunk), :], preferred_element_type=jnp.float32
             )
-            sums = both if sums is None else sums + both
             own = product if own is None else own + product
         own = own / jnp.sum(sums, axis=1, keepdims=True)
         peak = jnp.max(jnp.where(match, found, NEG_BIG), axis=1, keepdims=True)

time: 59 us -> 59 us (level)
  no operation moved by 1% of the time
where the time goes in v2:
time: 59 us; the launch traced here: 58.7 us
  starting transfers between devices  24.5 us (42%)
  Pallas kernels  19.5 us (33%)
  waiting for transfers between devices  13.2 us (22%)
  other arithmetic  0.83 us (1%)
  between operations  0.76 us (1%)
    ppermute x10, starting transfers between devices, beside(): return lax.ppermute(x, 'ulys', [(i, i ^ apart) for i in range(group)])  15.3 us
    ppermute x6, starting transfers between devices, onward(): return lax.ppermute(x, ('pipe', 'ulys'), pairs)  9.17 us
    pallas_call x3, Pallas kernels, stage(): pl.pallas_call(functools.partial(stage_kernel, head, span // pieces), out...  8.3 us
    pallas_call x2, Pallas kernels, attend(): pl.pallas_call(functools.partial(attend_kernel, order, [count for count,...  6.98 us
    ppermute x10, waiting for transfers between devices, beside(): return lax.ppermute(x, 'ulys', [(i, i ^ apart) for i in range(group)])  6.74 us
    ppermute x6, waiting for transfers between devices, onward(): return lax.ppermute(x, ('pipe', 'ulys'), pairs)  6.42 us
    pallas_call x2, Pallas kernels, project(): pl.pallas_call(functools.partial(project_kernel, parts, place), out_shape...  2.88 us
    pallas_call x1, Pallas kernels, modulate(): pl.pallas_call(modulate_kernel, out_shape=jax.ShapeDtypeStruct((tokens, w...  1.23 us
  transfers between devices with their start and end apart: 16, of which 6 were waited for; matrix products, arithmetic and copies ran while one was open for 0% of the time, Pallas kernels for 23%

profile of v2, /device:TPU:0, one launch (start us, length us, event | category | flops | bytes accessed | tf_op | source)
XLA Modules:
  0.0 58.7 jit_solution(8947832234847530962)
XLA Ops:
  0.0 1.2 %modulate.1.refs_0_ = bf16[32,3200]{1,0:T(8,128)(2,1)S(1)} custom-call(bf16[32,3072]{1,0:T(8,128)(2,1)} %bitcast.23, f32[3,1,3072]{2,1,0:T(1,128)} %bitcast.8, s32[1,32]{1,0:T(1,128)} %region_ref.1), custom_call_target="tpu_custom_call" | custom-call | tf_op jit(solution)/shard_map/modulate/pallas_call | solution.py:209
  1.2 4.1 %collective-permute-start.3 = (bf16[32,3200]{1,0:T(8,128)(2,1)S(1)}, bf16[32,3200]{1,0:T(8,128)(2,1)S(1)}, u32[]{:S(2)}, u32[]{:S(2)}) collective-permute-start(bf16[32,3200]{1,0:T(8,128)(2,1)S(1)} %modulate.1.refs_0_), channel_id=1, source_target_pairs={{0,4},{1,5},{2,6},{3,7},{4,0},{5,1},{6,2},{7,3},{8,12},{9,13},{10,... | collective-permute-start | bytes 614408 | tf_op jit(solution)/shard_map/ppermute | solution.py:449
  5.3 2.5 %collective-permute-start.2 = (bf16[32,3200]{1,0:T(8,128)(2,1)S(1)}, bf16[32,3200]{1,0:T(8,128)(2,1)S(1)}, u32[]{:S(2)}, u32[]{:S(2)}) collective-permute-start(bf16[32,3200]{1,0:T(8,128)(2,1)S(1)} %modulate.1.refs_0_), channel_id=1, source_target_pairs={{0,3},{1,2},{2,1},{3,0},{4,7},{5,6},{6,5},{7,4},{8,11},{9,10},{10,... | collective-permute-start | bytes 614408 | tf_op jit(solution)/shard_map/ppermute | solution.py:449
  7.9 0.4 collective-permute-start.1
  8.3 0.5 collective-permute-start
  8.8 2.8 %stage.4 = (bf16[128,3264]{1,0:T(8,128)(2,1)S(1)}, bf16[3264,128]{1,0:T(8,128)(2,1)S(1)}, bf16[3072,384]{1,0:T(8,128)(2,1)S(1)}, bf16[128,3072]{1,0:T(8,128)(2,1)S(1)}) custom-call(bf16[3072,2,384]{2,1,0:T(2,128)(2,1)} %bitcast.14, bf16[192,2,384]{2,1,0:T(2,128)(2,1)} %bitcast.20, bf16[3072,1152]{1,0:T(8,128)(2,1)} %bitcast.11, bf16[384,3072]{1,0:T(8,128)(2,1)} %bitcast.17), custom_call_target="tpu_custom_call" | custom-call | bytes 5652480 | tf_op jit(solution)/shard_map/stage/pallas_call | solution.py:260
  11.6 2.8 %stage.3 = (bf16[128,3264]{1,0:T(8,128)(2,1)S(1)}, bf16[3264,128]{1,0:T(8,128)(2,1)S(1)}, bf16[3072,384]{1,0:T(8,128)(2,1)S(1)}, bf16[128,3072]{1,0:T(8,128)(2,1)S(1)}) custom-call(bf16[3072,2,384]{2,1,0:T(2,128)(2,1)} %bitcast.15, bf16[192,2,384]{2,1,0:T(2,128)(2,1)} %bitcast.21, bf16[3072,1152]{1,0:T(8,128)(2,1)} %bitcast.12, bf16[384,3072]{1,0:T(8,128)(2,1)} %bitcast.18), custom_call_target="tpu_custom_call" | custom-call | bytes 5652480 | tf_op jit(solution)/shard_map/stage/pallas_call | solution.py:260
  14.4 0.5 collective-permute-done.3.refs_0_
  14.9 2.1 %collective-permute-start.6 = (bf16[32,3200]{1,0:T(8,128)(2,1)S(1)}, bf16[32,3200]{1,0:T(8,128)(2,1)S(1)}, u32[]{:S(2)}, u32[]{:S(2)}) collective-permute-start(bf16[32,3200]{1,0:T(8,128)(2,1)S(1)} %collective-permute-done.3.refs_0_), channel_id=1, source_target_pairs={{0,3},{1,2},{2,1},{3,0},{4,7},{5,6},{6,5},{7,4},{8,11},{9,10},{10,... | collective-permute-start | bytes 614408 | tf_op jit(solution)/shard_map/ppermute | solution.py:449
  17.0 0.9 %collective-permute-start.5 = (bf16[32,3200]{1,0:T(8,128)(2,1)S(1)}, bf16[32,3200]{1,0:T(8,128)(2,1)S(1)}, u32[]{:S(2)}, u32[]{:S(2)}) collective-permute-start(bf16[32,3200]{1,0:T(8,128)(2,1)S(1)} %collective-permute-done.3.refs_0_), channel_id=1, source_target_pairs={{0,2},{1,3},{2,0},{3,1},{4,6},{5,7},{6,4},{7,5},{8,10},{9,11},{10,... | collective-permute-start | bytes 614408 | tf_op jit(solution)/shard_map/ppermute | solution.py:449
  17.9 0.0 collective-permute-done.2.refs_3_
  17.9 1.1 %collective-permute-start.4 = (bf16[32,3200]{1,0:T(8,128)(2,1)S(1)}, bf16[32,3200]{1,0:T(8,128)(2,1)S(1)}, u32[]{:S(2)}, u32[]{:S(2)}) collective-permute-start(bf16[32,3200]{1,0:T(8,128)(2,1)S(1)} %collective-permute-done.3.refs_0_), channel_id=1, source_target_pairs={{0,1},{1,0},{2,3},{3,2},{4,5},{5,4},{6,7},{7,6},{8,9},{9,8},{10,11... | collective-permute-start | bytes 614408 | tf_op jit(solution)/shard_map/ppermute | solution.py:449
  19.0 2.8 %stage.5 = (bf16[128,3264]{1,0:T(8,128)(2,1)S(1)}, bf16[3264,128]{1,0:T(8,128)(2,1)S(1)}, bf16[3072,384]{1,0:T(8,128)(2,1)S(1)}, bf16[128,3072]{1,0:T(8,128)(2,1)S(1)}) custom-call(bf16[3072,2,384]{2,1,0:T(2,128)(2,1)} %bitcast.16, bf16[192,2,384]{2,1,0:T(2,128)(2,1)} %bitcast.22, bf16[3072,1152]{1,0:T(8,128)(2,1)} %bitcast.13, bf16[384,3072]{1,0:T(8,128)(2,1)} %bitcast.19), custom_call_target="tpu_custom_call" | custom-call | bytes 5652480 | tf_op jit(solution)/shard_map/stage/pallas_call | solution.py:260
  22.4 0.0 collective-permute-done.1.refs_2_
  22.4 0.0 collective-permute-done.refs_1_
  22.4 1.4 %project.2 = (bf16[128,384]{1,0:T(8,128)(2,1)S(1)}, bf16[128,128]{1,0:T(8,128)(2,1)S(1)}, bf16[128,3264]{1,0:T(8,128)(2,1)S(1)}, bf16[3264,128]{1,0:T(8,128)(2,1...) custom-call(s32[1]{0:T(128)S(6)} %copy.34.patch_ref, ...), custom_call_target="tpu_custom_call", output_to_operand_aliasing={{2}: (8, {}), {3}: (9, {}), {4}: (10, {}), {5}: (11, {}), {... | custom-call | flops 905969664 | bytes 8388608 | tf_op jit(solution)/shard_map/project/pallas_call | solution.py:311
  23.9 2.5 %collective-permute-done.6.refs_3_ = bf16[32,3200]{1,0:T(8,128)(2,1)S(1)} collective-permute-done((bf16[32,3200]{1,0:T(8,128)(2,1)S(1)}, bf16[32,3200]{1,0:T(8,128)(2,1)S(1)}, u32[]{:S(2)}, u32[]{:S(2)}) %collective-permute-start.6) | collective-permute-done | bytes 204832 | tf_op jit(solution)/shard_map/ppermute | solution.py:449
  26.3 2.9 %collective-permute-done.5.refs_2_ = bf16[32,3200]{1,0:T(8,128)(2,1)S(1)} collective-permute-done((bf16[32,3200]{1,0:T(8,128)(2,1)S(1)}, bf16[32,3200]{1,0:T(8,128)(2,1)S(1)}, u32[]{:S(2)}, u32[]{:S(2)}) %collective-permute-start.5) | collective-permute-done | bytes 204832 | tf_op jit(solution)/shard_map/ppermute | solution.py:449
  29.3 0.0 collective-permute-done.4.refs_1_
  29.3 0.0 copy-start
  29.3 0.0 copy-start.1
  29.3 1.4 %project.3 = (bf16[128,384]{1,0:T(8,128)(2,1)S(1)}, bf16[128,128]{1,0:T(8,128)(2,1)S(1)}, bf16[128,3264]{1,0:T(8,128)(2,1)S(1)}, bf16[3264,128]{1,0:T(8,128)(2,1...) custom-call(s32[1]{0:T(128)S(6)} %copy.34.patch_ref, ...), custom_call_target="tpu_custom_call", output_to_operand_aliasing={{2}: (8, {}), {3}: (9, {}), {4}: (10, {}), {5}: (11, {}), {... | custom-call | flops 905969664 | bytes 8388608 | tf_op jit(solution)/shard_map/project/pallas_call | solution.py:311
  30.7 0.0 copy-done
  30.7 0.0 copy-done.1
  30.8 3.5 %attend.2 = (f32[32,3072]{1,0:T(8,128)S(1)}, bf16[32,3072]{1,0:T(8,128)(2,1)S(1)}, bf16[32,3072]{1,0:T(8,128)(2,1)S(1)}, bf16[32,3072]{1,0:T(8,128)(2,1)S(1)}) custom-call(s32[1,6]{1,0:T(1,128)S(1)} %copy-done.1, f32[3,1,3072]{2,1,0:T(1,128)S(1)} %bitcast.9, bf16[128,384]{1,0:T(8,128)(2,1)S(1)} %get-tuple-element.103.refs_0_, ...), custom_call_target="tpu_custom_call" | custom-call | flops 905969664 | bytes 16777216 | tf_op jit(solution)/shard_map/attend/pallas_call | solution.py:400
  34.3 0.0 copy-start.2
  34.3 1.6 %collective-permute-start.11 = (bf16[32,3072]{1,0:T(8,128)(2,1)S(1)}, bf16[32,3072]{1,0:T(8,128)(2,1)S(1)}, u32[]{:S(2)}, u32[]{:S(2)}) collective-permute-start(bf16[32,3072]{1,0:T(8,128)(2,1)S(1)} %get-tuple-element.113), channel_id=1, source_target_pairs={{0,3},{1,2},{2,1},{3,0},{4,7},{5,6},{6,5},{7,4},{8,11},{9,10},{10,... | collective-permute-start | bytes 589832 | tf_op jit(solution)/shard_map/ppermute | solution.py:449
  35.9 0.5 collective-permute-start.12
  36.4 3.5 %attend.3 = (bf16[32,3072]{1,0:T(8,128)(2,1)S(1)}, bf16[32,3072]{1,0:T(8,128)(2,1)S(1)}, bf16[32,3072]{1,0:T(8,128)(2,1)S(1)}, bf16[32,3072]{1,0:T(8,128)(2,1)S(1)}) custom-call(s32[1,6]{1,0:T(1,128)S(1)} %copy-done.1, f32[3,1,3072]{2,1,0:T(1,128)S(1)} %bitcast.10, bf16[128,384]{1,0:T(8,128)(2,1)S(1)} %get-tuple-element.103.refs_0_, ...), custom_call_target="tpu_custom_call" | custom-call | flops 905969664 | bytes 16777216 | tf_op jit(solution)/shard_map/attend/pallas_call | solution.py:400
  39.9 1.5 %collective-permute-start.13 = (bf16[32,3072]{1,0:T(8,128)(2,1)S(1)}, bf16[32,3072]{1,0:T(8,128)(2,1)S(1)}, u32[]{:S(2)}, u32[]{:S(2)}) collective-permute-start(bf16[32,3072]{1,0:T(8,128)(2,1)S(1)} %get-tuple-element.115), channel_id=1, source_target_pairs={{0,2},{1,3},{2,0},{3,1},{4,6},{5,7},{6,4},{7,5},{8,10},{9,11},{10,... | collective-permute-start | bytes 589832 | tf_op jit(solution)/shard_map/ppermute | solution.py:449
  41.4 0.0 copy-done.2
  41.4 0.0 collective-permute-start.7
  41.4 2.7 %collective-permute-start.8 = (bf16[32,3072]{1,0:T(8,128)(2,1)S(1)}, bf16[32,3072]{1,0:T(8,128)(2,1)S(1)}, u32[]{:S(2)}, u32[]{:S(2)}) collective-permute-start(bf16[32,3072]{1,0:T(8,128)(2,1)S(1)} %get-tuple-element.109), channel_id=1, source_target_pairs={{0,11},{1,10},{2,9},{3,8},{4,15},{5,14},{6,13},{7,12},{8,19},{9,18... | collective-permute-start | bytes 589832 | tf_op jit(solution)/shard_map/ppermute | solution.py:457
  44.1 0.0 collective-permute-done.11.refs_0_
  44.1 0.0 collective-permute-start.9
  44.1 0.8 %collective-permute-done.12.refs_1_ = bf16[32,3072]{1,0:T(8,128)(2,1)S(1)} collective-permute-done((bf16[32,3072]{1,0:T(8,128)(2,1)S(1)}, bf16[32,3072]{1,0:T(8,128)(2,1)S(1)}, u32[]{:S(2)}, u32[]{:S(2)}) %collective-permute-start.12) | collective-permute-done | bytes 196640 | tf_op jit(solution)/shard_map/ppermute | solution.py:449
  44.9 0.9 %collective-permute-start.10 = (bf16[32,3072]{1,0:T(8,128)(2,1)S(1)}, bf16[32,3072]{1,0:T(8,128)(2,1)S(1)}, u32[]{:S(2)}, u32[]{:S(2)}) collective-permute-start(bf16[32,3072]{1,0:T(8,128)(2,1)S(1)} %get-tuple-element.111), channel_id=1, source_target_pairs={{0,10},{1,11},{2,8},{3,9},{4,14},{5,15},{6,12},{7,13},{8,18},{9,19... | collective-permute-start | bytes 589832 | tf_op jit(solution)/shard_map/ppermute | solution.py:457
  45.8 0.0 collective-permute-done.13.refs_2_
  45.8 0.1 add_terms.1
  45.9 2.8 %collective-permute-start.14 = (bf16[32,3072]{1,0:T(8,128)(2,1)S(1)}, bf16[32,3072]{1,0:T(8,128)(2,1)S(1)}, u32[]{:S(2)}, u32[]{:S(2)}) collective-permute-start(bf16[32,3072]{1,0:T(8,128)(2,1)S(1)} %add_terms.1), channel_id=1, source_target_pairs={{0,12},{1,13},{2,14},{3,15},{4,8},{5,9},{6,10},{7,11},{8,20},{9,21... | collective-permute-start | bytes 589832 | tf_op jit(solution)/shard_map/ppermute | solution.py:457
  48.8 0.0 collective-permute-done.7
  48.8 2.7 %collective-permute-start.15 = (bf16[32,3072]{1,0:T(8,128)(2,1)S(1)}, bf16[32,3072]{1,0:T(8,128)(2,1)S(1)}, u32[]{:S(2)}, u32[]{:S(2)}) collective-permute-start(bf16[32,3072]{1,0:T(8,128)(2,1)S(1)} %get-tuple-element.118), channel_id=1, source_target_pairs={{0,8},{1,9},{2,10},{3,11},{4,12},{5,13},{6,14},{7,15},{8,16},{9,17... | collective-permute-start | bytes 589832 | tf_op jit(solution)/shard_map/ppermute | solution.py:457
  51.5 0.0 collective-permute-done.8
  51.5 2.7 %collective-permute-done.9 = bf16[32,3072]{1,0:T(8,128)(2,1)S(1)} collective-permute-done((bf16[32,3072]{1,0:T(8,128)(2,1)S(1)}, bf16[32,3072]{1,0:T(8,128)(2,1)S(1)}, u32[]{:S(2)}, u32[]{:S(2)}) %collective-permute-start.9) | collective-permute-done | bytes 196640 | tf_op jit(solution)/shard_map/ppermute | solution.py:457
  54.1 3.7 %collective-permute-done.10 = bf16[32,3072]{1,0:T(8,128)(2,1)S(1)} collective-permute-done((bf16[32,3072]{1,0:T(8,128)(2,1)S(1)}, bf16[32,3072]{1,0:T(8,128)(2,1)S(1)}, u32[]{:S(2)}, u32[]{:S(2)}) %collective-permute-start.10) | collective-permute-done | bytes 196640 | tf_op jit(solution)/shard_map/ppermute | solution.py:457
  57.9 0.0 collective-permute-done.14
  57.9 0.0 collective-permute-done.15
  57.9 0.8 %fusion = bf16[1,32,3072]{2,1,0:T(8,128)(2,1)} fusion(bf16[32,3072]{1,0:T(8,128)(2,1)S(1)} %collective-permute-done.15, bf16[32,3072]{1,0:T(8,128)(2,1)S(1)} %collective-permute-done.14, bf16[32,3072]{1,0:T(8,128)(2,1)S(1)} %collective-permute-done.10, bf16[32,3072]{1,0:T(8,128)(2,1)S(1)} %collective-permute-done.9, ...), kind=kLoop, calls=%fused_computation.1 | loop fusion | flops 1179648 | bytes 1376256 | tf_op jit(solution)/shard_map/broadcast_in_dim | solution.py:497
Async XLA Ops:
  1.2 13.7 %collective-permute-start.3 = (bf16[32,3200]{1,0:T(8,128)(2,1)S(1)}, bf16[32,3200]{1,0:T(8,128)(2,1)S(1)}, u32[]{:S(2)}, u32[]{:S(2)}) collective-permute-start(bf16[32,3200]{1,0:T(8,128)(2,1)S(1)} %modulate.1.refs_0_), channel_id=1, source_target_pairs={{0,4},{1,5},{2,6},{3,7},{4,0},{5,1},{6,2},{7,3},{8,12},{9,13},{10,... | collective-permute-start | bytes 614408 | tf_op jit(solution)/shard_map/ppermute | solution.py:449
  5.3 12.6 %collective-permute-start.2 = (bf16[32,3200]{1,0:T(8,128)(2,1)S(1)}, bf16[32,3200]{1,0:T(8,128)(2,1)S(1)}, u32[]{:S(2)}, u32[]{:S(2)}) collective-permute-start(bf16[32,3200]{1,0:T(8,128)(2,1)S(1)} %modulate.1.refs_0_), channel_id=1, source_target_pairs={{0,3},{1,2},{2,1},{3,0},{4,7},{5,6},{6,5},{7,4},{8,11},{9,10},{10,... | collective-permute-start | bytes 614408 | tf_op jit(solution)/shard_map/ppermute | solution.py:449
  7.9 14.5 %collective-permute-start.1 = (bf16[32,3200]{1,0:T(8,128)(2,1)S(1)}, bf16[32,3200]{1,0:T(8,128)(2,1)S(1)}, u32[]{:S(2)}, u32[]{:S(2)}) collective-permute-start(bf16[32,3200]{1,0:T(8,128)(2,1)S(1)} %modulate.1.refs_0_), channel_id=1, source_target_pairs={{0,2},{1,3},{2,0},{3,1},{4,6},{5,7},{6,4},{7,5},{8,10},{9,11},{10,... | collective-permute-start | bytes 614408 | tf_op jit(solution)/shard_map/ppermute | solution.py:449
  8.3 14.1 %collective-permute-start = (bf16[32,3200]{1,0:T(8,128)(2,1)S(1)}, bf16[32,3200]{1,0:T(8,128)(2,1)S(1)}, u32[]{:S(2)}, u32[]{:S(2)}) collective-permute-start(bf16[32,3200]{1,0:T(8,128)(2,1)S(1)} %modulate.1.refs_0_), channel_id=1, source_target_pairs={{0,1},{1,0},{2,3},{3,2},{4,5},{5,4},{6,7},{7,6},{8,9},{9,8},{10,11... | collective-permute-start | bytes 614408 | tf_op jit(solution)/shard_map/ppermute | solution.py:449
  14.9 11.4 %collective-permute-start.6 = (bf16[32,3200]{1,0:T(8,128)(2,1)S(1)}, bf16[32,3200]{1,0:T(8,128)(2,1)S(1)}, u32[]{:S(2)}, u32[]{:S(2)}) collective-permute-start(bf16[32,3200]{1,0:T(8,128)(2,1)S(1)} %collective-permute-done.3.refs_0_), channel_id=1, source_target_pairs={{0,3},{1,2},{2,1},{3,0},{4,7},{5,6},{6,5},{7,4},{8,11},{9,10},{10,... | collective-permute-start | bytes 614408 | tf_op jit(solution)/shard_map/ppermute | solution.py:449
  17.0 12.3 %collective-permute-start.5 = (bf16[32,3200]{1,0:T(8,128)(2,1)S(1)}, bf16[32,3200]{1,0:T(8,128)(2,1)S(1)}, u32[]{:S(2)}, u32[]{:S(2)}) collective-permute-start(bf16[32,3200]{1,0:T(8,128)(2,1)S(1)} %collective-permute-done.3.refs_0_), channel_id=1, source_target_pairs={{0,2},{1,3},{2,0},{3,1},{4,6},{5,7},{6,4},{7,5},{8,10},{9,11},{10,... | collective-permute-start | bytes 614408 | tf_op jit(solution)/shard_map/ppermute | solution.py:449
  17.9 11.3 %collective-permute-start.4 = (bf16[32,3200]{1,0:T(8,128)(2,1)S(1)}, bf16[32,3200]{1,0:T(8,128)(2,1)S(1)}, u32[]{:S(2)}, u32[]{:S(2)}) collective-permute-start(bf16[32,3200]{1,0:T(8,128)(2,1)S(1)} %collective-permute-done.3.refs_0_), channel_id=1, source_target_pairs={{0,1},{1,0},{2,3},{3,2},{4,5},{5,4},{6,7},{7,6},{8,9},{9,8},{10,11... | collective-permute-start | bytes 614408 | tf_op jit(solution)/shard_map/ppermute | solution.py:449
  29.3 1.4 %copy-start = (f32[1,3,3072]{2,0,1:T(1,128)S(1)}, f32[1,3,3072]{2,0,1:T(1,128)}, u32[]{:S(2)}) copy-start(f32[1,3,3072]{2,0,1:T(1,128)} %param.11) | copy-start | bytes 110596
  29.3 1.5 %copy-start.1 = (s32[1,6]{1,0:T(1,128)S(1)}, s32[1,6]{1,0:T(1,128)}, u32[]{:S(2)}) copy-start(s32[1,6]{1,0:T(1,128)} %counts_ref.3) | copy-start | bytes 76
  34.3 7.1 %copy-start.2 = (bf16[1,32,3072]{2,1,0:T(8,128)(2,1)S(1)}, bf16[1,32,3072]{2,1,0:T(8,128)(2,1)}, u32[]{:S(2)}) copy-start(bf16[1,32,3072]{2,1,0:T(8,128)(2,1)} %param.9) | copy-start | bytes 589828
  34.3 9.9 %collective-permute-start.11 = (bf16[32,3072]{1,0:T(8,128)(2,1)S(1)}, bf16[32,3072]{1,0:T(8,128)(2,1)S(1)}, u32[]{:S(2)}, u32[]{:S(2)}) collective-permute-start(bf16[32,3072]{1,0:T(8,128)(2,1)S(1)} %get-tuple-element.113), channel_id=1, source_target_pairs={{0,3},{1,2},{2,1},{3,0},{4,7},{5,6},{6,5},{7,4},{8,11},{9,10},{10,... | collective-permute-start | bytes 589832 | tf_op jit(solution)/shard_map/ppermute | solution.py:449
  35.9 9.0 %collective-permute-start.12 = (bf16[32,3072]{1,0:T(8,128)(2,1)S(1)}, bf16[32,3072]{1,0:T(8,128)(2,1)S(1)}, u32[]{:S(2)}, u32[]{:S(2)}) collective-permute-start(bf16[32,3072]{1,0:T(8,128)(2,1)S(1)} %get-tuple-element.114), channel_id=1, source_target_pairs={{0,1},{1,0},{2,3},{3,2},{4,5},{5,4},{6,7},{7,6},{8,9},{9,8},{10,11... | collective-permute-start | bytes 589832 | tf_op jit(solution)/shard_map/ppermute | solution.py:449
  39.9 6.0 %collective-permute-start.13 = (bf16[32,3072]{1,0:T(8,128)(2,1)S(1)}, bf16[32,3072]{1,0:T(8,128)(2,1)S(1)}, u32[]{:S(2)}, u32[]{:S(2)}) collective-permute-start(bf16[32,3072]{1,0:T(8,128)(2,1)S(1)} %get-tuple-element.115), channel_id=1, source_target_pairs={{0,2},{1,3},{2,0},{3,1},{4,6},{5,7},{6,4},{7,5},{8,10},{9,11},{10,... | collective-permute-start | bytes 589832 | tf_op jit(solution)/shard_map/ppermute | solution.py:449
  41.4 7.4 %collective-permute-start.7 = (bf16[32,3072]{1,0:T(8,128)(2,1)S(1)}, bf16[32,3072]{1,0:T(8,128)(2,1)S(1)}, u32[]{:S(2)}, u32[]{:S(2)}) collective-permute-start(bf16[32,3072]{1,0:T(8,128)(2,1)S(1)} %bitcast.24), channel_id=1, source_target_pairs={{0,8},{1,9},{2,10},{3,11},{4,12},{5,13},{6,14},{7,15},{8,16},{9,17... | collective-permute-start | bytes 589832 | tf_op jit(solution)/shard_map/ppermute | solution.py:457
  41.4 10.1 %collective-permute-start.8 = (bf16[32,3072]{1,0:T(8,128)(2,1)S(1)}, bf16[32,3072]{1,0:T(8,128)(2,1)S(1)}, u32[]{:S(2)}, u32[]{:S(2)}) collective-permute-start(bf16[32,3072]{1,0:T(8,128)(2,1)S(1)} %get-tuple-element.109), channel_id=1, source_target_pairs={{0,11},{1,10},{2,9},{3,8},{4,15},{5,14},{6,13},{7,12},{8,19},{9,18... | collective-permute-start | bytes 589832 | tf_op jit(solution)/shard_map/ppermute | solution.py:457
  44.1 10.0 %collective-permute-start.9 = (bf16[32,3072]{1,0:T(8,128)(2,1)S(1)}, bf16[32,3072]{1,0:T(8,128)(2,1)S(1)}, u32[]{:S(2)}, u32[]{:S(2)}) collective-permute-start(bf16[32,3072]{1,0:T(8,128)(2,1)S(1)} %get-tuple-element.110), channel_id=1, source_target_pairs={{0,9},{1,8},{2,11},{3,10},{4,13},{5,12},{6,15},{7,14},{8,17},{9,16... | collective-permute-start | bytes 589832 | tf_op jit(solution)/shard_map/ppermute | solution.py:457
  44.9 13.0 %collective-permute-start.10 = (bf16[32,3072]{1,0:T(8,128)(2,1)S(1)}, bf16[32,3072]{1,0:T(8,128)(2,1)S(1)}, u32[]{:S(2)}, u32[]{:S(2)}) collective-permute-start(bf16[32,3072]{1,0:T(8,128)(2,1)S(1)} %get-tuple-element.111), channel_id=1, source_target_pairs={{0,10},{1,11},{2,8},{3,9},{4,14},{5,15},{6,12},{7,13},{8,18},{9,19... | collective-permute-start | bytes 589832 | tf_op jit(solution)/shard_map/ppermute | solution.py:457
  45.9 12.0 %collective-permute-start.14 = (bf16[32,3072]{1,0:T(8,128)(2,1)S(1)}, bf16[32,3072]{1,0:T(8,128)(2,1)S(1)}, u32[]{:S(2)}, u32[]{:S(2)}) collective-permute-start(bf16[32,3072]{1,0:T(8,128)(2,1)S(1)} %add_terms.1), channel_id=1, source_target_pairs={{0,12},{1,13},{2,14},{3,15},{4,8},{5,9},{6,10},{7,11},{8,20},{9,21... | collective-permute-start | bytes 589832 | tf_op jit(solution)/shard_map/ppermute | solution.py:457
  48.8 9.1 %collective-permute-start.15 = (bf16[32,3072]{1,0:T(8,128)(2,1)S(1)}, bf16[32,3072]{1,0:T(8,128)(2,1)S(1)}, u32[]{:S(2)}, u32[]{:S(2)}) collective-permute-start(bf16[32,3072]{1,0:T(8,128)(2,1)S(1)} %get-tuple-element.118), channel_id=1, source_target_pairs={{0,8},{1,9},{2,10},{3,11},{4,12},{5,13},{6,14},{7,15},{8,16},{9,17... | collective-permute-start | bytes 589832 | tf_op jit(solution)/shard_map/ppermute | solution.py:457

commit v3 on v1

--- a/solution.py
+++ b/solution.py
@@ -465,7 +465,7 @@
     b0 = modulate(rows, modul, region_ids)
     b4, b1, b3, b2 = (beside(b0, r) for r in (4, 1, 3, 2))
     heads = [staged(h) for h in range(HPD)]
-    b4, *early = hold((b4, *heads[0], *heads[1]))
+    b4, b1, *early = hold((b4, b1, *heads[0], *heads[1]))
     heads[0], heads[1] = early[: len(heads[0])], early[len(heads[0]) :]
     b7, b5, b6 = beside(b4, 3), beside(b4, 1), beside(b4, 2)
     weights, fields = [head[2] for head in heads], [array for head in heads for array in head[:2]]
@@ -485,8 +485,8 @@
     t4, t7, t5, t6 = attended((4, 7, 5, 6), [wide] + [narrow] * 3, queries=(query_near, query_far))
     t4, t7, t5, t6, query_near = hold((t4, t7, t5, t6, query_near))
     t3, t1, t2, t0 = attended((3, 1, 2, 0), [narrow] * 4, queries=(query_near, query_far))
+    t7, rows = hold((t7, rows))
     c7, c5, c6 = beside(t7, 3), beside(t5, 1), beside(t6, 2)
-    rows, t3, t1, t2, t0 = hold((rows, t3, t1, t2, t0))
     before = onward(rows, 0)
     c3, c1, c2 = onward(t3, 3), onward(t1, 1), onward(t2, 2)
     s4 = add_terms(t4, c7, c5, c6)

time: 59 us -> 59.4 us (level)
  waiting for transfers between devices: 13.2 us -> 15.2 us
  starting transfers between devices: 24.4 us -> 22.7 us
    ppermute x6, waiting for transfers between devices: 6.42 us -> 8.4 us  [onward(): return lax.ppermute(x, ('pipe', 'ulys'), pairs)]
    ppermute x6, starting transfers between devices: 9.15 us -> 8.06 us  [onward(): return lax.ppermute(x, ('pipe', 'ulys'), pairs)]
    ppermute x10, starting transfers between devices: 15.3 us -> 14.6 us  [beside(): return lax.ppermute(x, 'ulys', [(i, i ^ apart) for i in range(group)])]
where the time goes in v3:
time: 59.4 us; the launch traced here: 59 us
  starting transfers between devices  22.7 us (38%)
  Pallas kernels  19.4 us (33%)
  waiting for transfers between devices  15.2 us (26%)
  other arithmetic  0.83 us (1%)
  between operations  0.77 us (1%)
    ppermute x10, starting transfers between devices, beside(): return lax.ppermute(x, 'ulys', [(i, i ^ apart) for i in range(group)])  14.6 us
    ppermute x6, waiting for transfers between devices, onward(): return lax.ppermute(x, ('pipe', 'ulys'), pairs)  8.4 us
    pallas_call x3, Pallas kernels, stage(): pl.pallas_call(functools.partial(stage_kernel, head, span // pieces), out...  8.3 us
    ppermute x6, starting transfers between devices, onward(): return lax.ppermute(x, ('pipe', 'ulys'), pairs)  8.06 us
    pallas_call x2, Pallas kernels, attend(): pl.pallas_call(functools.partial(attend_kernel, order, [count for count,...  6.94 us
    ppermute x10, waiting for transfers between devices, beside(): return lax.ppermute(x, 'ulys', [(i, i ^ apart) for i in range(group)])  6.85 us
    pallas_call x2, Pallas kernels, project(): pl.pallas_call(functools.partial(project_kernel, parts, place), out_shape...  2.87 us
    pallas_call x1, Pallas kernels, modulate(): pl.pallas_call(modulate_kernel, out_shape=jax.ShapeDtypeStruct((tokens, w...  1.23 us
  transfers between devices with their start and end apart: 16, of which 6 were waited for; matrix products, arithmetic and copies ran while one was open for 0% of the time, Pallas kernels for 23%

profile of v3, /device:TPU:0, one launch (start us, length us, event | category | flops | bytes accessed | tf_op | source)
XLA Modules:
  0.0 59.0 jit_solution(14876050078386073386)
XLA Ops:
  0.0 1.2 %modulate.1.refs_0_ = bf16[32,3200]{1,0:T(8,128)(2,1)S(1)} custom-call(bf16[32,3072]{1,0:T(8,128)(2,1)} %bitcast.23, f32[3,1,3072]{2,1,0:T(1,128)} %bitcast.8, s32[1,32]{1,0:T(1,128)} %region_ref.1), custom_call_target="tpu_custom_call" | custom-call | tf_op jit(solution)/shard_map/modulate/pallas_call | solution.py:209
  1.2 3.0 %collective-permute-start.1 = (bf16[32,3200]{1,0:T(8,128)(2,1)S(1)}, bf16[32,3200]{1,0:T(8,128)(2,1)S(1)}, u32[]{:S(2)}, u32[]{:S(2)}) collective-permute-start(bf16[32,3200]{1,0:T(8,128)(2,1)S(1)} %modulate.1.refs_0_), channel_id=1, source_target_pairs={{0,1},{1,0},{2,3},{3,2},{4,5},{5,4},{6,7},{7,6},{8,9},{9,8},{10,11... | collective-permute-start | bytes 614408 | tf_op jit(solution)/shard_map/ppermute | solution.py:447
  4.3 2.6 %collective-permute-start = (bf16[32,3200]{1,0:T(8,128)(2,1)S(1)}, bf16[32,3200]{1,0:T(8,128)(2,1)S(1)}, u32[]{:S(2)}, u32[]{:S(2)}) collective-permute-start(bf16[32,3200]{1,0:T(8,128)(2,1)S(1)} %modulate.1.refs_0_), channel_id=1, source_target_pairs={{0,4},{1,5},{2,6},{3,7},{4,0},{5,1},{6,2},{7,3},{8,12},{9,13},{10,... | collective-permute-start | bytes 614408 | tf_op jit(solution)/shard_map/ppermute | solution.py:447
  6.9 1.5 %collective-permute-start.3 = (bf16[32,3200]{1,0:T(8,128)(2,1)S(1)}, bf16[32,3200]{1,0:T(8,128)(2,1)S(1)}, u32[]{:S(2)}, u32[]{:S(2)}) collective-permute-start(bf16[32,3200]{1,0:T(8,128)(2,1)S(1)} %modulate.1.refs_0_), channel_id=1, source_target_pairs={{0,3},{1,2},{2,1},{3,0},{4,7},{5,6},{6,5},{7,4},{8,11},{9,10},{10,... | collective-permute-start | bytes 614408 | tf_op jit(solution)/shard_map/ppermute | solution.py:447
  8.4 0.4 collective-permute-start.2
  8.8 2.8 %stage.4 = (bf16[128,3264]{1,0:T(8,128)(2,1)S(1)}, bf16[3264,128]{1,0:T(8,128)(2,1)S(1)}, bf16[3072,384]{1,0:T(8,128)(2,1)S(1)}, bf16[128,3072]{1,0:T(8,128)(2,1)S(1)}) custom-call(bf16[3072,2,384]{2,1,0:T(2,128)(2,1)} %bitcast.14, bf16[192,2,384]{2,1,0:T(2,128)(2,1)} %bitcast.20, bf16[3072,1152]{1,0:T(8,128)(2,1)} %bitcast.11, bf16[384,3072]{1,0:T(8,128)(2,1)} %bitcast.17), custom_call_target="tpu_custom_call" | custom-call | bytes 5652480 | tf_op jit(solution)/shard_map/stage/pallas_call | solution.py:260
  11.6 2.8 %stage.3 = (bf16[128,3264]{1,0:T(8,128)(2,1)S(1)}, bf16[3264,128]{1,0:T(8,128)(2,1)S(1)}, bf16[3072,384]{1,0:T(8,128)(2,1)S(1)}, bf16[128,3072]{1,0:T(8,128)(2,1)S(1)}) custom-call(bf16[3072,2,384]{2,1,0:T(2,128)(2,1)} %bitcast.15, bf16[192,2,384]{2,1,0:T(2,128)(2,1)} %bitcast.21, bf16[3072,1152]{1,0:T(8,128)(2,1)} %bitcast.12, bf16[384,3072]{1,0:T(8,128)(2,1)} %bitcast.18), custom_call_target="tpu_custom_call" | custom-call | bytes 5652480 | tf_op jit(solution)/shard_map/stage/pallas_call | solution.py:260
  14.4 0.0 collective-permute-done.1.refs_1_
  14.4 1.8 %collective-permute-done.refs_0_ = bf16[32,3200]{1,0:T(8,128)(2,1)S(1)} collective-permute-done((bf16[32,3200]{1,0:T(8,128)(2,1)S(1)}, bf16[32,3200]{1,0:T(8,128)(2,1)S(1)}, u32[]{:S(2)}, u32[]{:S(2)}) %collective-permute-start) | collective-permute-done | bytes 204832 | tf_op jit(solution)/shard_map/ppermute | solution.py:447
  16.2 0.8 %collective-permute-start.6 = (bf16[32,3200]{1,0:T(8,128)(2,1)S(1)}, bf16[32,3200]{1,0:T(8,128)(2,1)S(1)}, u32[]{:S(2)}, u32[]{:S(2)}) collective-permute-start(bf16[32,3200]{1,0:T(8,128)(2,1)S(1)} %collective-permute-done.refs_0_), channel_id=1, source_target_pairs={{0,3},{1,2},{2,1},{3,0},{4,7},{5,6},{6,5},{7,4},{8,11},{9,10},{10,... | collective-permute-start | bytes 614408 | tf_op jit(solution)/shard_map/ppermute | solution.py:447
  17.0 1.1 %collective-permute-start.5 = (bf16[32,3200]{1,0:T(8,128)(2,1)S(1)}, bf16[32,3200]{1,0:T(8,128)(2,1)S(1)}, u32[]{:S(2)}, u32[]{:S(2)}) collective-permute-start(bf16[32,3200]{1,0:T(8,128)(2,1)S(1)} %collective-permute-done.refs_0_), channel_id=1, source_target_pairs={{0,2},{1,3},{2,0},{3,1},{4,6},{5,7},{6,4},{7,5},{8,10},{9,11},{10,... | collective-permute-start | bytes 614408 | tf_op jit(solution)/shard_map/ppermute | solution.py:447
  18.1 1.6 %collective-permute-start.4 = (bf16[32,3200]{1,0:T(8,128)(2,1)S(1)}, bf16[32,3200]{1,0:T(8,128)(2,1)S(1)}, u32[]{:S(2)}, u32[]{:S(2)}) collective-permute-start(bf16[32,3200]{1,0:T(8,128)(2,1)S(1)} %collective-permute-done.refs_0_), channel_id=1, source_target_pairs={{0,1},{1,0},{2,3},{3,2},{4,5},{5,4},{6,7},{7,6},{8,9},{9,8},{10,11... | collective-permute-start | bytes 614408 | tf_op jit(solution)/shard_map/ppermute | solution.py:447
  19.7 2.8 %stage.5 = (bf16[128,3264]{1,0:T(8,128)(2,1)S(1)}, bf16[3264,128]{1,0:T(8,128)(2,1)S(1)}, bf16[3072,384]{1,0:T(8,128)(2,1)S(1)}, bf16[128,3072]{1,0:T(8,128)(2,1)S(1)}) custom-call(bf16[3072,2,384]{2,1,0:T(2,128)(2,1)} %bitcast.16, bf16[192,2,384]{2,1,0:T(2,128)(2,1)} %bitcast.22, bf16[3072,1152]{1,0:T(8,128)(2,1)} %bitcast.13, bf16[384,3072]{1,0:T(8,128)(2,1)} %bitcast.19), custom_call_target="tpu_custom_call" | custom-call | bytes 5652480 | tf_op jit(solution)/shard_map/stage/pallas_call | solution.py:260
  23.1 0.0 collective-permute-done.3.refs_3_
  23.1 0.0 collective-permute-done.2.refs_2_
  23.1 1.4 %project.2 = (bf16[128,384]{1,0:T(8,128)(2,1)S(1)}, bf16[128,128]{1,0:T(8,128)(2,1)S(1)}, bf16[128,3264]{1,0:T(8,128)(2,1)S(1)}, bf16[3264,128]{1,0:T(8,128)(2,1...) custom-call(s32[1]{0:T(128)S(6)} %copy.34.patch_ref, ...), custom_call_target="tpu_custom_call", output_to_operand_aliasing={{2}: (8, {}), {3}: (9, {}), {4}: (10, {}), {5}: (11, {}), {... | custom-call | flops 905969664 | bytes 8388608 | tf_op jit(solution)/shard_map/project/pallas_call | solution.py:311
  24.6 3.2 %collective-permute-done.6.refs_3_ = bf16[32,3200]{1,0:T(8,128)(2,1)S(1)} collective-permute-done((bf16[32,3200]{1,0:T(8,128)(2,1)S(1)}, bf16[32,3200]{1,0:T(8,128)(2,1)S(1)}, u32[]{:S(2)}, u32[]{:S(2)}) %collective-permute-start.6) | collective-permute-done | bytes 204832 | tf_op jit(solution)/shard_map/ppermute | solution.py:447
  27.8 1.8 %collective-permute-done.5.refs_2_ = bf16[32,3200]{1,0:T(8,128)(2,1)S(1)} collective-permute-done((bf16[32,3200]{1,0:T(8,128)(2,1)S(1)}, bf16[32,3200]{1,0:T(8,128)(2,1)S(1)}, u32[]{:S(2)}, u32[]{:S(2)}) %collective-permute-start.5) | collective-permute-done | bytes 204832 | tf_op jit(solution)/shard_map/ppermute | solution.py:447
  29.6 0.0 collective-permute-done.4.refs_1_
  29.6 0.0 copy-start
  29.6 0.0 copy-start.1
  29.6 1.4 %project.3 = (bf16[128,384]{1,0:T(8,128)(2,1)S(1)}, bf16[128,128]{1,0:T(8,128)(2,1)S(1)}, bf16[128,3264]{1,0:T(8,128)(2,1)S(1)}, bf16[3264,128]{1,0:T(8,128)(2,1...) custom-call(s32[1]{0:T(128)S(6)} %copy.34.patch_ref, ...), custom_call_target="tpu_custom_call", output_to_operand_aliasing={{2}: (8, {}), {3}: (9, {}), {4}: (10, {}), {5}: (11, {}), {... | custom-call | flops 905969664 | bytes 8388608 | tf_op jit(solution)/shard_map/project/pallas_call | solution.py:311
  31.0 0.0 copy-done
  31.0 0.0 copy-done.1
  31.1 0.0 copy-start.2
  31.1 3.5 %attend.2 = (f32[32,3072]{1,0:T(8,128)S(1)}, bf16[32,3072]{1,0:T(8,128)(2,1)S(1)}, bf16[32,3072]{1,0:T(8,128)(2,1)S(1)}, bf16[32,3072]{1,0:T(8,128)(2,1)S(1)}) custom-call(s32[1,6]{1,0:T(1,128)S(1)} %copy-done.1, f32[3,1,3072]{2,1,0:T(1,128)S(1)} %bitcast.9, bf16[128,384]{1,0:T(8,128)(2,1)S(1)} %get-tuple-element.104.refs_0_, ...), custom_call_target="tpu_custom_call" | custom-call | flops 905969664 | bytes 16777216 | tf_op jit(solution)/shard_map/attend/pallas_call | solution.py:398
  34.5 1.4 %collective-permute-start.11 = (bf16[32,3072]{1,0:T(8,128)(2,1)S(1)}, bf16[32,3072]{1,0:T(8,128)(2,1)S(1)}, u32[]{:S(2)}, u32[]{:S(2)}) collective-permute-start(bf16[32,3072]{1,0:T(8,128)(2,1)S(1)} %get-tuple-element.109), channel_id=1, source_target_pairs={{0,3},{1,2},{2,1},{3,0},{4,7},{5,6},{6,5},{7,4},{8,11},{9,10},{10,... | collective-permute-start | bytes 589832 | tf_op jit(solution)/shard_map/ppermute | solution.py:447
  36.0 1.5 %collective-permute-start.12 = (bf16[32,3072]{1,0:T(8,128)(2,1)S(1)}, bf16[32,3072]{1,0:T(8,128)(2,1)S(1)}, u32[]{:S(2)}, u32[]{:S(2)}) collective-permute-start(bf16[32,3072]{1,0:T(8,128)(2,1)S(1)} %get-tuple-element.110), channel_id=1, source_target_pairs={{0,1},{1,0},{2,3},{3,2},{4,5},{5,4},{6,7},{7,6},{8,9},{9,8},{10,11... | collective-permute-start | bytes 589832 | tf_op jit(solution)/shard_map/ppermute | solution.py:447
  37.5 0.6 collective-permute-start.13
  38.1 0.0 copy-done.2
  38.1 0.0 collective-permute-start.7
  38.1 3.5 %attend.3 = (bf16[32,3072]{1,0:T(8,128)(2,1)S(1)}, bf16[32,3072]{1,0:T(8,128)(2,1)S(1)}, bf16[32,3072]{1,0:T(8,128)(2,1)S(1)}, bf16[32,3072]{1,0:T(8,128)(2,1)S(1)}) custom-call(s32[1,6]{1,0:T(1,128)S(1)} %copy-done.1, f32[3,1,3072]{2,1,0:T(1,128)S(1)} %bitcast.10, bf16[128,384]{1,0:T(8,128)(2,1)S(1)} %get-tuple-element.104.refs_0_, ...), custom_call_target="tpu_custom_call" | custom-call | flops 905969664 | bytes 16777216 | tf_op jit(solution)/shard_map/attend/pallas_call | solution.py:398
  41.6 2.7 %collective-permute-start.8 = (bf16[32,3072]{1,0:T(8,128)(2,1)S(1)}, bf16[32,3072]{1,0:T(8,128)(2,1)S(1)}, u32[]{:S(2)}, u32[]{:S(2)}) collective-permute-start(bf16[32,3072]{1,0:T(8,128)(2,1)S(1)} %get-tuple-element.105), channel_id=1, source_target_pairs={{0,11},{1,10},{2,9},{3,8},{4,15},{5,14},{6,13},{7,12},{8,19},{9,18... | collective-permute-start | bytes 589832 | tf_op jit(solution)/shard_map/ppermute | solution.py:455
  44.3 0.0 collective-permute-done.11.refs_0_
  44.3 0.9 %collective-permute-start.9 = (bf16[32,3072]{1,0:T(8,128)(2,1)S(1)}, bf16[32,3072]{1,0:T(8,128)(2,1)S(1)}, u32[]{:S(2)}, u32[]{:S(2)}) collective-permute-start(bf16[32,3072]{1,0:T(8,128)(2,1)S(1)} %get-tuple-element.106), channel_id=1, source_target_pairs={{0,9},{1,8},{2,11},{3,10},{4,13},{5,12},{6,15},{7,14},{8,17},{9,16... | collective-permute-start | bytes 589832 | tf_op jit(solution)/shard_map/ppermute | solution.py:455
  45.2 0.0 collective-permute-done.12.refs_1_
  45.2 0.8 %collective-permute-start.10 = (bf16[32,3072]{1,0:T(8,128)(2,1)S(1)}, bf16[32,3072]{1,0:T(8,128)(2,1)S(1)}, u32[]{:S(2)}, u32[]{:S(2)}) collective-permute-start(bf16[32,3072]{1,0:T(8,128)(2,1)S(1)} %get-tuple-element.107), channel_id=1, source_target_pairs={{0,10},{1,11},{2,8},{3,9},{4,14},{5,15},{6,12},{7,13},{8,18},{9,19... | collective-permute-start | bytes 589832 | tf_op jit(solution)/shard_map/ppermute | solution.py:455
  46.0 0.0 collective-permute-done.13.refs_2_
  46.0 0.1 add_terms.1
  46.1 3.6 %collective-permute-start.14 = (bf16[32,3072]{1,0:T(8,128)(2,1)S(1)}, bf16[32,3072]{1,0:T(8,128)(2,1)S(1)}, u32[]{:S(2)}, u32[]{:S(2)}) collective-permute-start(bf16[32,3072]{1,0:T(8,128)(2,1)S(1)} %add_terms.1), channel_id=1, source_target_pairs={{0,12},{1,13},{2,14},{3,15},{4,8},{5,9},{6,10},{7,11},{8,20},{9,21... | collective-permute-start | bytes 589832 | tf_op jit(solution)/shard_map/ppermute | solution.py:455
  49.7 0.0 collective-permute-done.7
  49.7 0.0 collective-permute-start.15
  49.7 0.7 %collective-permute-done.8 = bf16[32,3072]{1,0:T(8,128)(2,1)S(1)} collective-permute-done((bf16[32,3072]{1,0:T(8,128)(2,1)S(1)}, bf16[32,3072]{1,0:T(8,128)(2,1)S(1)}, u32[]{:S(2)}, u32[]{:S(2)}) %collective-permute-start.8) | collective-permute-done | bytes 196640 | tf_op jit(solution)/shard_map/ppermute | solution.py:455
  50.5 3.2 %collective-permute-done.9 = bf16[32,3072]{1,0:T(8,128)(2,1)S(1)} collective-permute-done((bf16[32,3072]{1,0:T(8,128)(2,1)S(1)}, bf16[32,3072]{1,0:T(8,128)(2,1)S(1)}, u32[]{:S(2)}, u32[]{:S(2)}) %collective-permute-start.9) | collective-permute-done | bytes 196640 | tf_op jit(solution)/shard_map/ppermute | solution.py:455
  53.6 4.5 %collective-permute-done.10 = bf16[32,3072]{1,0:T(8,128)(2,1)S(1)} collective-permute-done((bf16[32,3072]{1,0:T(8,128)(2,1)S(1)}, bf16[32,3072]{1,0:T(8,128)(2,1)S(1)}, u32[]{:S(2)}, u32[]{:S(2)}) %collective-permute-start.10) | collective-permute-done | bytes 196640 | tf_op jit(solution)/shard_map/ppermute | solution.py:455
  58.1 0.0 collective-permute-done.14
  58.1 0.0 collective-permute-done.15
  58.1 0.8 %fusion = bf16[1,32,3072]{2,1,0:T(8,128)(2,1)} fusion(bf16[32,3072]{1,0:T(8,128)(2,1)S(1)} %collective-permute-done.15, bf16[32,3072]{1,0:T(8,128)(2,1)S(1)} %collective-permute-done.14, bf16[32,3072]{1,0:T(8,128)(2,1)S(1)} %collective-permute-done.10, bf16[32,3072]{1,0:T(8,128)(2,1)S(1)} %collective-permute-done.9, ...), kind=kLoop, calls=%fused_computation.1 | loop fusion | flops 1179648 | bytes 1376256 | tf_op jit(solution)/shard_map/broadcast_in_dim | solution.py:495
Async XLA Ops:
  1.2 13.2 %collective-permute-start.1 = (bf16[32,3200]{1,0:T(8,128)(2,1)S(1)}, bf16[32,3200]{1,0:T(8,128)(2,1)S(1)}, u32[]{:S(2)}, u32[]{:S(2)}) collective-permute-start(bf16[32,3200]{1,0:T(8,128)(2,1)S(1)} %modulate.1.refs_0_), channel_id=1, source_target_pairs={{0,1},{1,0},{2,3},{3,2},{4,5},{5,4},{6,7},{7,6},{8,9},{9,8},{10,11... | collective-permute-start | bytes 614408 | tf_op jit(solution)/shard_map/ppermute | solution.py:447
  4.3 11.9 %collective-permute-start = (bf16[32,3200]{1,0:T(8,128)(2,1)S(1)}, bf16[32,3200]{1,0:T(8,128)(2,1)S(1)}, u32[]{:S(2)}, u32[]{:S(2)}) collective-permute-start(bf16[32,3200]{1,0:T(8,128)(2,1)S(1)} %modulate.1.refs_0_), channel_id=1, source_target_pairs={{0,4},{1,5},{2,6},{3,7},{4,0},{5,1},{6,2},{7,3},{8,12},{9,13},{10,... | collective-permute-start | bytes 614408 | tf_op jit(solution)/shard_map/ppermute | solution.py:447
  6.9 16.2 %collective-permute-start.3 = (bf16[32,3200]{1,0:T(8,128)(2,1)S(1)}, bf16[32,3200]{1,0:T(8,128)(2,1)S(1)}, u32[]{:S(2)}, u32[]{:S(2)}) collective-permute-start(bf16[32,3200]{1,0:T(8,128)(2,1)S(1)} %modulate.1.refs_0_), channel_id=1, source_target_pairs={{0,3},{1,2},{2,1},{3,0},{4,7},{5,6},{6,5},{7,4},{8,11},{9,10},{10,... | collective-permute-start | bytes 614408 | tf_op jit(solution)/shard_map/ppermute | solution.py:447
  8.4 14.7 %collective-permute-start.2 = (bf16[32,3200]{1,0:T(8,128)(2,1)S(1)}, bf16[32,3200]{1,0:T(8,128)(2,1)S(1)}, u32[]{:S(2)}, u32[]{:S(2)}) collective-permute-start(bf16[32,3200]{1,0:T(8,128)(2,1)S(1)} %modulate.1.refs_0_), channel_id=1, source_target_pairs={{0,2},{1,3},{2,0},{3,1},{4,6},{5,7},{6,4},{7,5},{8,10},{9,11},{10,... | collective-permute-start | bytes 614408 | tf_op jit(solution)/shard_map/ppermute | solution.py:447
  16.2 11.6 %collective-permute-start.6 = (bf16[32,3200]{1,0:T(8,128)(2,1)S(1)}, bf16[32,3200]{1,0:T(8,128)(2,1)S(1)}, u32[]{:S(2)}, u32[]{:S(2)}) collective-permute-start(bf16[32,3200]{1,0:T(8,128)(2,1)S(1)} %collective-permute-done.refs_0_), channel_id=1, source_target_pairs={{0,3},{1,2},{2,1},{3,0},{4,7},{5,6},{6,5},{7,4},{8,11},{9,10},{10,... | collective-permute-start | bytes 614408 | tf_op jit(solution)/shard_map/ppermute | solution.py:447
  17.0 12.6 %collective-permute-start.5 = (bf16[32,3200]{1,0:T(8,128)(2,1)S(1)}, bf16[32,3200]{1,0:T(8,128)(2,1)S(1)}, u32[]{:S(2)}, u32[]{:S(2)}) collective-permute-start(bf16[32,3200]{1,0:T(8,128)(2,1)S(1)} %collective-permute-done.refs_0_), channel_id=1, source_target_pairs={{0,2},{1,3},{2,0},{3,1},{4,6},{5,7},{6,4},{7,5},{8,10},{9,11},{10,... | collective-permute-start | bytes 614408 | tf_op jit(solution)/shard_map/ppermute | solution.py:447
  18.1 11.5 %collective-permute-start.4 = (bf16[32,3200]{1,0:T(8,128)(2,1)S(1)}, bf16[32,3200]{1,0:T(8,128)(2,1)S(1)}, u32[]{:S(2)}, u32[]{:S(2)}) collective-permute-start(bf16[32,3200]{1,0:T(8,128)(2,1)S(1)} %collective-permute-done.refs_0_), channel_id=1, source_target_pairs={{0,1},{1,0},{2,3},{3,2},{4,5},{5,4},{6,7},{7,6},{8,9},{9,8},{10,11... | collective-permute-start | bytes 614408 | tf_op jit(solution)/shard_map/ppermute | solution.py:447
  29.6 1.4 %copy-start = (f32[1,3,3072]{2,0,1:T(1,128)S(1)}, f32[1,3,3072]{2,0,1:T(1,128)}, u32[]{:S(2)}) copy-start(f32[1,3,3072]{2,0,1:T(1,128)} %param.11) | copy-start | bytes 110596
  29.6 1.4 %copy-start.1 = (s32[1,6]{1,0:T(1,128)S(1)}, s32[1,6]{1,0:T(1,128)}, u32[]{:S(2)}) copy-start(s32[1,6]{1,0:T(1,128)} %counts_ref.3) | copy-start | bytes 76
  31.1 7.0 %copy-start.2 = (bf16[1,32,3072]{2,1,0:T(8,128)(2,1)S(1)}, bf16[1,32,3072]{2,1,0:T(8,128)(2,1)}, u32[]{:S(2)}) copy-start(bf16[1,32,3072]{2,1,0:T(8,128)(2,1)} %param.9) | copy-start | bytes 589828
  34.5 9.7 %collective-permute-start.11 = (bf16[32,3072]{1,0:T(8,128)(2,1)S(1)}, bf16[32,3072]{1,0:T(8,128)(2,1)S(1)}, u32[]{:S(2)}, u32[]{:S(2)}) collective-permute-start(bf16[32,3072]{1,0:T(8,128)(2,1)S(1)} %get-tuple-element.109), channel_id=1, source_target_pairs={{0,3},{1,2},{2,1},{3,0},{4,7},{5,6},{6,5},{7,4},{8,11},{9,10},{10,... | collective-permute-start | bytes 589832 | tf_op jit(solution)/shard_map/ppermute | solution.py:447
  36.0 9.2 %collective-permute-start.12 = (bf16[32,3072]{1,0:T(8,128)(2,1)S(1)}, bf16[32,3072]{1,0:T(8,128)(2,1)S(1)}, u32[]{:S(2)}, u32[]{:S(2)}) collective-permute-start(bf16[32,3072]{1,0:T(8,128)(2,1)S(1)} %get-tuple-element.110), channel_id=1, source_target_pairs={{0,1},{1,0},{2,3},{3,2},{4,5},{5,4},{6,7},{7,6},{8,9},{9,8},{10,11... | collective-permute-start | bytes 589832 | tf_op jit(solution)/shard_map/ppermute | solution.py:447
  37.5 8.5 %collective-permute-start.13 = (bf16[32,3072]{1,0:T(8,128)(2,1)S(1)}, bf16[32,3072]{1,0:T(8,128)(2,1)S(1)}, u32[]{:S(2)}, u32[]{:S(2)}) collective-permute-start(bf16[32,3072]{1,0:T(8,128)(2,1)S(1)} %get-tuple-element.111), channel_id=1, source_target_pairs={{0,2},{1,3},{2,0},{3,1},{4,6},{5,7},{6,4},{7,5},{8,10},{9,11},{10,... | collective-permute-start | bytes 589832 | tf_op jit(solution)/shard_map/ppermute | solution.py:447
  38.1 11.6 %collective-permute-start.7 = (bf16[32,3072]{1,0:T(8,128)(2,1)S(1)}, bf16[32,3072]{1,0:T(8,128)(2,1)S(1)}, u32[]{:S(2)}, u32[]{:S(2)}) collective-permute-start(bf16[32,3072]{1,0:T(8,128)(2,1)S(1)} %bitcast.24), channel_id=1, source_target_pairs={{0,8},{1,9},{2,10},{3,11},{4,12},{5,13},{6,14},{7,15},{8,16},{9,17... | collective-permute-start | bytes 589832 | tf_op jit(solution)/shard_map/ppermute | solution.py:455
  41.6 8.9 %collective-permute-start.8 = (bf16[32,3072]{1,0:T(8,128)(2,1)S(1)}, bf16[32,3072]{1,0:T(8,128)(2,1)S(1)}, u32[]{:S(2)}, u32[]{:S(2)}) collective-permute-start(bf16[32,3072]{1,0:T(8,128)(2,1)S(1)} %get-tuple-element.105), channel_id=1, source_target_pairs={{0,11},{1,10},{2,9},{3,8},{4,15},{5,14},{6,13},{7,12},{8,19},{9,18... | collective-permute-start | bytes 589832 | tf_op jit(solution)/shard_map/ppermute | solution.py:455
  44.3 9.4 %collective-permute-start.9 = (bf16[32,3072]{1,0:T(8,128)(2,1)S(1)}, bf16[32,3072]{1,0:T(8,128)(2,1)S(1)}, u32[]{:S(2)}, u32[]{:S(2)}) collective-permute-start(bf16[32,3072]{1,0:T(8,128)(2,1)S(1)} %get-tuple-element.106), channel_id=1, source_target_pairs={{0,9},{1,8},{2,11},{3,10},{4,13},{5,12},{6,15},{7,14},{8,17},{9,16... | collective-permute-start | bytes 589832 | tf_op jit(solution)/shard_map/ppermute | solution.py:455
  45.2 12.9 %collective-permute-start.10 = (bf16[32,3072]{1,0:T(8,128)(2,1)S(1)}, bf16[32,3072]{1,0:T(8,128)(2,1)S(1)}, u32[]{:S(2)}, u32[]{:S(2)}) collective-permute-start(bf16[32,3072]{1,0:T(8,128)(2,1)S(1)} %get-tuple-element.107), channel_id=1, source_target_pairs={{0,10},{1,11},{2,8},{3,9},{4,14},{5,15},{6,12},{7,13},{8,18},{9,19... | collective-permute-start | bytes 589832 | tf_op jit(solution)/shard_map/ppermute | solution.py:455
  46.1 12.0 %collective-permute-start.14 = (bf16[32,3072]{1,0:T(8,128)(2,1)S(1)}, bf16[32,3072]{1,0:T(8,128)(2,1)S(1)}, u32[]{:S(2)}, u32[]{:S(2)}) collective-permute-start(bf16[32,3072]{1,0:T(8,128)(2,1)S(1)} %add_terms.1), channel_id=1, source_target_pairs={{0,12},{1,13},{2,14},{3,15},{4,8},{5,9},{6,10},{7,11},{8,20},{9,21... | collective-permute-start | bytes 589832 | tf_op jit(solution)/shard_map/ppermute | solution.py:455
  49.7 8.4 %collective-permute-start.15 = (bf16[32,3072]{1,0:T(8,128)(2,1)S(1)}, bf16[32,3072]{1,0:T(8,128)(2,1)S(1)}, u32[]{:S(2)}, u32[]{:S(2)}) collective-permute-start(bf16[32,3072]{1,0:T(8,128)(2,1)S(1)} %get-tuple-element.114), channel_id=1, source_target_pairs={{0,8},{1,9},{2,10},{3,11},{4,12},{5,13},{6,14},{7,15},{8,16},{9,17... | collective-permute-start | bytes 589832 | tf_op jit(solution)/shard_map/ppermute | solution.py:455

commit v4 on v1

--- a/solution.py
+++ b/solution.py
@@ -488,10 +488,10 @@
     c7, c5, c6 = beside(t7, 3), beside(t5, 1), beside(t6, 2)
     rows, t3, t1, t2, t0 = hold((rows, t3, t1, t2, t0))
     before = onward(rows, 0)
-    c3, c1, c2 = onward(t3, 3), onward(t1, 1), onward(t2, 2)
+    c3, c1 = onward(t3, 3), onward(t1, 1)
     s4 = add_terms(t4, c7, c5, c6)
-    s4, t0 = hold((s4, t0))
-    parts = before, c3, c1, c2, onward(s4, 4), onward(t0, 0)
+    s4, t0, t2 = hold((s4, t0, t2))
+    parts = before, c3, c1, onward(s4, 4), onward(t2, 2), onward(t0, 0)
     return sum(part.astype(jnp.float32) for part in parts).astype(jnp.bfloat16)[None]
 
 

time: 59 us -> 59.3 us (level)
  waiting for transfers between devices: 13.2 us -> 16.3 us
  starting transfers between devices: 24.4 us -> 21.8 us
    ppermute x6, waiting for transfers between devices: 6.42 us -> 9.6 us  [onward(): return lax.ppermute(x, ('pipe', 'ulys'), pairs)]
    ppermute x6, starting transfers between devices: 9.15 us -> 6.55 us  [onward(): return lax.ppermute(x, ('pipe', 'ulys'), pairs)]
  transfers between devices with their start and end apart: 16 -> 16, of which waited for: 6 -> 7; matrix products, arithmetic and copies ran while one was open for 0% -> 0% of each run, Pallas kernels for 23% -> 22%
where the time goes in v4:
time: 59.3 us; the launch traced here: 59.2 us
  starting transfers between devices  21.8 us (37%)
  Pallas kernels  19.4 us (33%)
  waiting for transfers between devices  16.3 us (27%)
  other arithmetic  0.84 us (1%)
  between operations  0.77 us (1%)
    ppermute x10, starting transfers between devices, beside(): return lax.ppermute(x, 'ulys', [(i, i ^ apart) for i in range(group)])  15.2 us
    ppermute x6, waiting for transfers between devices, onward(): return lax.ppermute(x, ('pipe', 'ulys'), pairs)  9.6 us
    pallas_call x3, Pallas kernels, stage(): pl.pallas_call(functools.partial(stage_kernel, head, span // pieces), out...  8.3 us
    pallas_call x2, Pallas kernels, attend(): pl.pallas_call(functools.partial(attend_kernel, order, [count for count,...  6.94 us
    ppermute x10, waiting for transfers between devices, beside(): return lax.ppermute(x, 'ulys', [(i, i ^ apart) for i in range(group)])  6.73 us
    ppermute x6, starting transfers between devices, onward(): return lax.ppermute(x, ('pipe', 'ulys'), pairs)  6.55 us
    pallas_call x2, Pallas kernels, project(): pl.pallas_call(functools.partial(project_kernel, parts, place), out_shape...  2.88 us
    pallas_call x1, Pallas kernels, modulate(): pl.pallas_call(modulate_kernel, out_shape=jax.ShapeDtypeStruct((tokens, w...  1.23 us
  transfers between devices with their start and end apart: 16, of which 7 were waited for; matrix products, arithmetic and copies ran while one was open for 0% of the time, Pallas kernels for 22%

profile of v4, /device:TPU:0, one launch (start us, length us, event | category | flops | bytes accessed | tf_op | source)
XLA Modules:
  0.0 59.2 jit_solution(14283459283980931992)
XLA Ops:
  0.0 1.2 %modulate.1.refs_0_ = bf16[32,3200]{1,0:T(8,128)(2,1)S(1)} custom-call(bf16[32,3072]{1,0:T(8,128)(2,1)} %bitcast.23, f32[3,1,3072]{2,1,0:T(1,128)} %bitcast.8, s32[1,32]{1,0:T(1,128)} %region_ref.1), custom_call_target="tpu_custom_call" | custom-call | tf_op jit(solution)/shard_map/modulate/pallas_call | solution.py:209
  1.2 4.1 %collective-permute-start.3 = (bf16[32,3200]{1,0:T(8,128)(2,1)S(1)}, bf16[32,3200]{1,0:T(8,128)(2,1)S(1)}, u32[]{:S(2)}, u32[]{:S(2)}) collective-permute-start(bf16[32,3200]{1,0:T(8,128)(2,1)S(1)} %modulate.1.refs_0_), channel_id=1, source_target_pairs={{0,4},{1,5},{2,6},{3,7},{4,0},{5,1},{6,2},{7,3},{8,12},{9,13},{10,... | collective-permute-start | bytes 614408 | tf_op jit(solution)/shard_map/ppermute | solution.py:447
  5.3 2.5 %collective-permute-start.2 = (bf16[32,3200]{1,0:T(8,128)(2,1)S(1)}, bf16[32,3200]{1,0:T(8,128)(2,1)S(1)}, u32[]{:S(2)}, u32[]{:S(2)}) collective-permute-start(bf16[32,3200]{1,0:T(8,128)(2,1)S(1)} %modulate.1.refs_0_), channel_id=1, source_target_pairs={{0,3},{1,2},{2,1},{3,0},{4,7},{5,6},{6,5},{7,4},{8,11},{9,10},{10,... | collective-permute-start | bytes 614408 | tf_op jit(solution)/shard_map/ppermute | solution.py:447
  7.9 0.4 collective-permute-start.1
  8.3 0.5 collective-permute-start
  8.8 2.8 %stage.4 = (bf16[128,3264]{1,0:T(8,128)(2,1)S(1)}, bf16[3264,128]{1,0:T(8,128)(2,1)S(1)}, bf16[3072,384]{1,0:T(8,128)(2,1)S(1)}, bf16[128,3072]{1,0:T(8,128)(2,1)S(1)}) custom-call(bf16[3072,2,384]{2,1,0:T(2,128)(2,1)} %bitcast.14, bf16[192,2,384]{2,1,0:T(2,128)(2,1)} %bitcast.20, bf16[3072,1152]{1,0:T(8,128)(2,1)} %bitcast.11, bf16[384,3072]{1,0:T(8,128)(2,1)} %bitcast.17), custom_call_target="tpu_custom_call" | custom-call | bytes 5652480 | tf_op jit(solution)/shard_map/stage/pallas_call | solution.py:260
  11.6 2.8 %stage.3 = (bf16[128,3264]{1,0:T(8,128)(2,1)S(1)}, bf16[3264,128]{1,0:T(8,128)(2,1)S(1)}, bf16[3072,384]{1,0:T(8,128)(2,1)S(1)}, bf16[128,3072]{1,0:T(8,128)(2,1)S(1)}) custom-call(bf16[3072,2,384]{2,1,0:T(2,128)(2,1)} %bitcast.15, bf16[192,2,384]{2,1,0:T(2,128)(2,1)} %bitcast.21, bf16[3072,1152]{1,0:T(8,128)(2,1)} %bitcast.12, bf16[384,3072]{1,0:T(8,128)(2,1)} %bitcast.18), custom_call_target="tpu_custom_call" | custom-call | bytes 5652480 | tf_op jit(solution)/shard_map/stage/pallas_call | solution.py:260
  14.4 0.5 collective-permute-done.3.refs_0_
  14.9 2.1 %collective-permute-start.6 = (bf16[32,3200]{1,0:T(8,128)(2,1)S(1)}, bf16[32,3200]{1,0:T(8,128)(2,1)S(1)}, u32[]{:S(2)}, u32[]{:S(2)}) collective-permute-start(bf16[32,3200]{1,0:T(8,128)(2,1)S(1)} %collective-permute-done.3.refs_0_), channel_id=1, source_target_pairs={{0,3},{1,2},{2,1},{3,0},{4,7},{5,6},{6,5},{7,4},{8,11},{9,10},{10,... | collective-permute-start | bytes 614408 | tf_op jit(solution)/shard_map/ppermute | solution.py:447
  17.0 0.9 %collective-permute-start.5 = (bf16[32,3200]{1,0:T(8,128)(2,1)S(1)}, bf16[32,3200]{1,0:T(8,128)(2,1)S(1)}, u32[]{:S(2)}, u32[]{:S(2)}) collective-permute-start(bf16[32,3200]{1,0:T(8,128)(2,1)S(1)} %collective-permute-done.3.refs_0_), channel_id=1, source_target_pairs={{0,2},{1,3},{2,0},{3,1},{4,6},{5,7},{6,4},{7,5},{8,10},{9,11},{10,... | collective-permute-start | bytes 614408 | tf_op jit(solution)/shard_map/ppermute | solution.py:447
  17.9 0.0 collective-permute-done.2.refs_3_
  17.9 1.1 %collective-permute-start.4 = (bf16[32,3200]{1,0:T(8,128)(2,1)S(1)}, bf16[32,3200]{1,0:T(8,128)(2,1)S(1)}, u32[]{:S(2)}, u32[]{:S(2)}) collective-permute-start(bf16[32,3200]{1,0:T(8,128)(2,1)S(1)} %collective-permute-done.3.refs_0_), channel_id=1, source_target_pairs={{0,1},{1,0},{2,3},{3,2},{4,5},{5,4},{6,7},{7,6},{8,9},{9,8},{10,11... | collective-permute-start | bytes 614408 | tf_op jit(solution)/shard_map/ppermute | solution.py:447
  19.0 2.8 %stage.5 = (bf16[128,3264]{1,0:T(8,128)(2,1)S(1)}, bf16[3264,128]{1,0:T(8,128)(2,1)S(1)}, bf16[3072,384]{1,0:T(8,128)(2,1)S(1)}, bf16[128,3072]{1,0:T(8,128)(2,1)S(1)}) custom-call(bf16[3072,2,384]{2,1,0:T(2,128)(2,1)} %bitcast.16, bf16[192,2,384]{2,1,0:T(2,128)(2,1)} %bitcast.22, bf16[3072,1152]{1,0:T(8,128)(2,1)} %bitcast.13, bf16[384,3072]{1,0:T(8,128)(2,1)} %bitcast.19), custom_call_target="tpu_custom_call" | custom-call | bytes 5652480 | tf_op jit(solution)/shard_map/stage/pallas_call | solution.py:260
  22.4 0.0 collective-permute-done.1.refs_2_
  22.4 0.0 collective-permute-done.refs_1_
  22.4 1.4 %project.2 = (bf16[128,384]{1,0:T(8,128)(2,1)S(1)}, bf16[128,128]{1,0:T(8,128)(2,1)S(1)}, bf16[128,3264]{1,0:T(8,128)(2,1)S(1)}, bf16[3264,128]{1,0:T(8,128)(2,1...) custom-call(s32[1]{0:T(128)S(6)} %copy.34.patch_ref, ...), custom_call_target="tpu_custom_call", output_to_operand_aliasing={{2}: (8, {}), {3}: (9, {}), {4}: (10, {}), {5}: (11, {}), {... | custom-call | flops 905969664 | bytes 8388608 | tf_op jit(solution)/shard_map/project/pallas_call | solution.py:311
  23.9 2.5 %collective-permute-done.6.refs_3_ = bf16[32,3200]{1,0:T(8,128)(2,1)S(1)} collective-permute-done((bf16[32,3200]{1,0:T(8,128)(2,1)S(1)}, bf16[32,3200]{1,0:T(8,128)(2,1)S(1)}, u32[]{:S(2)}, u32[]{:S(2)}) %collective-permute-start.6) | collective-permute-done | bytes 204832 | tf_op jit(solution)/shard_map/ppermute | solution.py:447
  26.3 2.9 %collective-permute-done.5.refs_2_ = bf16[32,3200]{1,0:T(8,128)(2,1)S(1)} collective-permute-done((bf16[32,3200]{1,0:T(8,128)(2,1)S(1)}, bf16[32,3200]{1,0:T(8,128)(2,1)S(1)}, u32[]{:S(2)}, u32[]{:S(2)}) %collective-permute-start.5) | collective-permute-done | bytes 204832 | tf_op jit(solution)/shard_map/ppermute | solution.py:447
  29.3 0.0 collective-permute-done.4.refs_1_
  29.3 0.0 copy-start
  29.3 0.0 copy-start.1
  29.3 1.4 %project.3 = (bf16[128,384]{1,0:T(8,128)(2,1)S(1)}, bf16[128,128]{1,0:T(8,128)(2,1)S(1)}, bf16[128,3264]{1,0:T(8,128)(2,1)S(1)}, bf16[3264,128]{1,0:T(8,128)(2,1...) custom-call(s32[1]{0:T(128)S(6)} %copy.34.patch_ref, ...), custom_call_target="tpu_custom_call", output_to_operand_aliasing={{2}: (8, {}), {3}: (9, {}), {4}: (10, {}), {5}: (11, {}), {... | custom-call | flops 905969664 | bytes 8388608 | tf_op jit(solution)/shard_map/project/pallas_call | solution.py:311
  30.7 0.0 copy-done
  30.7 0.0 copy-done.1
  30.8 3.5 %attend.2 = (f32[32,3072]{1,0:T(8,128)S(1)}, bf16[32,3072]{1,0:T(8,128)(2,1)S(1)}, bf16[32,3072]{1,0:T(8,128)(2,1)S(1)}, bf16[32,3072]{1,0:T(8,128)(2,1)S(1)}) custom-call(s32[1,6]{1,0:T(1,128)S(1)} %copy-done.1, f32[3,1,3072]{2,1,0:T(1,128)S(1)} %bitcast.9, bf16[128,384]{1,0:T(8,128)(2,1)S(1)} %get-tuple-element.104.refs_0_, ...), custom_call_target="tpu_custom_call" | custom-call | flops 905969664 | bytes 16777216 | tf_op jit(solution)/shard_map/attend/pallas_call | solution.py:398
  34.2 0.0 copy-start.2
  34.3 1.6 %collective-permute-start.10 = (bf16[32,3072]{1,0:T(8,128)(2,1)S(1)}, bf16[32,3072]{1,0:T(8,128)(2,1)S(1)}, u32[]{:S(2)}, u32[]{:S(2)}) collective-permute-start(bf16[32,3072]{1,0:T(8,128)(2,1)S(1)} %get-tuple-element.113), channel_id=1, source_target_pairs={{0,3},{1,2},{2,1},{3,0},{4,7},{5,6},{6,5},{7,4},{8,11},{9,10},{10,... | collective-permute-start | bytes 589832 | tf_op jit(solution)/shard_map/ppermute | solution.py:447
  35.8 0.5 collective-permute-start.11
  36.3 1.5 %collective-permute-start.12 = (bf16[32,3072]{1,0:T(8,128)(2,1)S(1)}, bf16[32,3072]{1,0:T(8,128)(2,1)S(1)}, u32[]{:S(2)}, u32[]{:S(2)}) collective-permute-start(bf16[32,3072]{1,0:T(8,128)(2,1)S(1)} %get-tuple-element.115), channel_id=1, source_target_pairs={{0,2},{1,3},{2,0},{3,1},{4,6},{5,7},{6,4},{7,5},{8,10},{9,11},{10,... | collective-permute-start | bytes 589832 | tf_op jit(solution)/shard_map/ppermute | solution.py:447
  37.8 3.5 %attend.3 = (bf16[32,3072]{1,0:T(8,128)(2,1)S(1)}, bf16[32,3072]{1,0:T(8,128)(2,1)S(1)}, bf16[32,3072]{1,0:T(8,128)(2,1)S(1)}, bf16[32,3072]{1,0:T(8,128)(2,1)S(1)}) custom-call(s32[1,6]{1,0:T(1,128)S(1)} %copy-done.1, f32[3,1,3072]{2,1,0:T(1,128)S(1)} %bitcast.10, bf16[128,384]{1,0:T(8,128)(2,1)S(1)} %get-tuple-element.104.refs_0_, ...), custom_call_target="tpu_custom_call" | custom-call | flops 905969664 | bytes 16777216 | tf_op jit(solution)/shard_map/attend/pallas_call | solution.py:398
  41.3 0.0 copy-done.2
  41.3 0.1 collective-permute-start.7
  41.4 2.7 %collective-permute-start.8 = (bf16[32,3072]{1,0:T(8,128)(2,1)S(1)}, bf16[32,3072]{1,0:T(8,128)(2,1)S(1)}, u32[]{:S(2)}, u32[]{:S(2)}) collective-permute-start(bf16[32,3072]{1,0:T(8,128)(2,1)S(1)} %get-tuple-element.110), channel_id=1, source_target_pairs={{0,11},{1,10},{2,9},{3,8},{4,15},{5,14},{6,13},{7,12},{8,19},{9,18... | collective-permute-start | bytes 589832 | tf_op jit(solution)/shard_map/ppermute | solution.py:455
  44.1 0.0 collective-permute-done.10.refs_0_
  44.1 0.0 collective-permute-start.9
  44.1 0.8 %collective-permute-done.11.refs_1_ = bf16[32,3072]{1,0:T(8,128)(2,1)S(1)} collective-permute-done((bf16[32,3072]{1,0:T(8,128)(2,1)S(1)}, bf16[32,3072]{1,0:T(8,128)(2,1)S(1)}, u32[]{:S(2)}, u32[]{:S(2)}) %collective-permute-start.11) | collective-permute-done | bytes 196640 | tf_op jit(solution)/shard_map/ppermute | solution.py:447
  44.9 0.0 collective-permute-done.12.refs_2_
  44.9 0.1 add_terms.1
  45.0 2.0 %collective-permute-start.13 = (bf16[32,3072]{1,0:T(8,128)(2,1)S(1)}, bf16[32,3072]{1,0:T(8,128)(2,1)S(1)}, u32[]{:S(2)}, u32[]{:S(2)}) collective-permute-start(bf16[32,3072]{1,0:T(8,128)(2,1)S(1)} %add_terms.1), channel_id=1, source_target_pairs={{0,12},{1,13},{2,14},{3,15},{4,8},{5,9},{6,10},{7,11},{8,20},{9,21... | collective-permute-start | bytes 589832 | tf_op jit(solution)/shard_map/ppermute | solution.py:455
  46.9 1.8 %collective-permute-start.14 = (bf16[32,3072]{1,0:T(8,128)(2,1)S(1)}, bf16[32,3072]{1,0:T(8,128)(2,1)S(1)}, u32[]{:S(2)}, u32[]{:S(2)}) collective-permute-start(bf16[32,3072]{1,0:T(8,128)(2,1)S(1)} %get-tuple-element.119), channel_id=1, source_target_pairs={{0,10},{1,11},{2,8},{3,9},{4,14},{5,15},{6,12},{7,13},{8,18},{9,19... | collective-permute-start | bytes 589832 | tf_op jit(solution)/shard_map/ppermute | solution.py:455
  48.7 0.0 collective-permute-done.7
  48.7 0.0 collective-permute-start.15
  48.7 1.6 %collective-permute-done.8 = bf16[32,3072]{1,0:T(8,128)(2,1)S(1)} collective-permute-done((bf16[32,3072]{1,0:T(8,128)(2,1)S(1)}, bf16[32,3072]{1,0:T(8,128)(2,1)S(1)}, u32[]{:S(2)}, u32[]{:S(2)}) %collective-permute-start.8) | collective-permute-done | bytes 196640 | tf_op jit(solution)/shard_map/ppermute | solution.py:455
  50.3 3.0 %collective-permute-done.9 = bf16[32,3072]{1,0:T(8,128)(2,1)S(1)} collective-permute-done((bf16[32,3072]{1,0:T(8,128)(2,1)S(1)}, bf16[32,3072]{1,0:T(8,128)(2,1)S(1)}, u32[]{:S(2)}, u32[]{:S(2)}) %collective-permute-start.9) | collective-permute-done | bytes 196640 | tf_op jit(solution)/shard_map/ppermute | solution.py:455
  53.3 5.0 %collective-permute-done.13 = bf16[32,3072]{1,0:T(8,128)(2,1)S(1)} collective-permute-done((bf16[32,3072]{1,0:T(8,128)(2,1)S(1)}, bf16[32,3072]{1,0:T(8,128)(2,1)S(1)}, u32[]{:S(2)}, u32[]{:S(2)}) %collective-permute-start.13) | collective-permute-done | bytes 196640 | tf_op jit(solution)/shard_map/ppermute | solution.py:455
  58.3 0.0 collective-permute-done.14
  58.3 0.0 collective-permute-done.15
  58.3 0.8 %fusion = bf16[1,32,3072]{2,1,0:T(8,128)(2,1)} fusion(bf16[32,3072]{1,0:T(8,128)(2,1)S(1)} %collective-permute-done.15, bf16[32,3072]{1,0:T(8,128)(2,1)S(1)} %collective-permute-done.14, bf16[32,3072]{1,0:T(8,128)(2,1)S(1)} %collective-permute-done.13, bf16[32,3072]{1,0:T(8,128)(2,1)S(1)} %collective-permute-done.9, ...), kind=kLoop, calls=%fused_computation.1 | loop fusion | flops 1179648 | bytes 1376256 | tf_op jit(solution)/shard_map/broadcast_in_dim | solution.py:495
Async XLA Ops:
  1.2 13.7 %collective-permute-start.3 = (bf16[32,3200]{1,0:T(8,128)(2,1)S(1)}, bf16[32,3200]{1,0:T(8,128)(2,1)S(1)}, u32[]{:S(2)}, u32[]{:S(2)}) collective-permute-start(bf16[32,3200]{1,0:T(8,128)(2,1)S(1)} %modulate.1.refs_0_), channel_id=1, source_target_pairs={{0,4},{1,5},{2,6},{3,7},{4,0},{5,1},{6,2},{7,3},{8,12},{9,13},{10,... | collective-permute-start | bytes 614408 | tf_op jit(solution)/shard_map/ppermute | solution.py:447
  5.3 12.6 %collective-permute-start.2 = (bf16[32,3200]{1,0:T(8,128)(2,1)S(1)}, bf16[32,3200]{1,0:T(8,128)(2,1)S(1)}, u32[]{:S(2)}, u32[]{:S(2)}) collective-permute-start(bf16[32,3200]{1,0:T(8,128)(2,1)S(1)} %modulate.1.refs_0_), channel_id=1, source_target_pairs={{0,3},{1,2},{2,1},{3,0},{4,7},{5,6},{6,5},{7,4},{8,11},{9,10},{10,... | collective-permute-start | bytes 614408 | tf_op jit(solution)/shard_map/ppermute | solution.py:447
  7.9 14.5 %collective-permute-start.1 = (bf16[32,3200]{1,0:T(8,128)(2,1)S(1)}, bf16[32,3200]{1,0:T(8,128)(2,1)S(1)}, u32[]{:S(2)}, u32[]{:S(2)}) collective-permute-start(bf16[32,3200]{1,0:T(8,128)(2,1)S(1)} %modulate.1.refs_0_), channel_id=1, source_target_pairs={{0,2},{1,3},{2,0},{3,1},{4,6},{5,7},{6,4},{7,5},{8,10},{9,11},{10,... | collective-permute-start | bytes 614408 | tf_op jit(solution)/shard_map/ppermute | solution.py:447
  8.3 14.1 %collective-permute-start = (bf16[32,3200]{1,0:T(8,128)(2,1)S(1)}, bf16[32,3200]{1,0:T(8,128)(2,1)S(1)}, u32[]{:S(2)}, u32[]{:S(2)}) collective-permute-start(bf16[32,3200]{1,0:T(8,128)(2,1)S(1)} %modulate.1.refs_0_), channel_id=1, source_target_pairs={{0,1},{1,0},{2,3},{3,2},{4,5},{5,4},{6,7},{7,6},{8,9},{9,8},{10,11... | collective-permute-start | bytes 614408 | tf_op jit(solution)/shard_map/ppermute | solution.py:447
  14.9 11.4 %collective-permute-start.6 = (bf16[32,3200]{1,0:T(8,128)(2,1)S(1)}, bf16[32,3200]{1,0:T(8,128)(2,1)S(1)}, u32[]{:S(2)}, u32[]{:S(2)}) collective-permute-start(bf16[32,3200]{1,0:T(8,128)(2,1)S(1)} %collective-permute-done.3.refs_0_), channel_id=1, source_target_pairs={{0,3},{1,2},{2,1},{3,0},{4,7},{5,6},{6,5},{7,4},{8,11},{9,10},{10,... | collective-permute-start | bytes 614408 | tf_op jit(solution)/shard_map/ppermute | solution.py:447
  17.0 12.3 %collective-permute-start.5 = (bf16[32,3200]{1,0:T(8,128)(2,1)S(1)}, bf16[32,3200]{1,0:T(8,128)(2,1)S(1)}, u32[]{:S(2)}, u32[]{:S(2)}) collective-permute-start(bf16[32,3200]{1,0:T(8,128)(2,1)S(1)} %collective-permute-done.3.refs_0_), channel_id=1, source_target_pairs={{0,2},{1,3},{2,0},{3,1},{4,6},{5,7},{6,4},{7,5},{8,10},{9,11},{10,... | collective-permute-start | bytes 614408 | tf_op jit(solution)/shard_map/ppermute | solution.py:447
  17.9 11.3 %collective-permute-start.4 = (bf16[32,3200]{1,0:T(8,128)(2,1)S(1)}, bf16[32,3200]{1,0:T(8,128)(2,1)S(1)}, u32[]{:S(2)}, u32[]{:S(2)}) collective-permute-start(bf16[32,3200]{1,0:T(8,128)(2,1)S(1)} %collective-permute-done.3.refs_0_), channel_id=1, source_target_pairs={{0,1},{1,0},{2,3},{3,2},{4,5},{5,4},{6,7},{7,6},{8,9},{9,8},{10,11... | collective-permute-start | bytes 614408 | tf_op jit(solution)/shard_map/ppermute | solution.py:447
  29.3 1.4 %copy-start = (f32[1,3,3072]{2,0,1:T(1,128)S(1)}, f32[1,3,3072]{2,0,1:T(1,128)}, u32[]{:S(2)}) copy-start(f32[1,3,3072]{2,0,1:T(1,128)} %param.11) | copy-start | bytes 110596
  29.3 1.5 %copy-start.1 = (s32[1,6]{1,0:T(1,128)S(1)}, s32[1,6]{1,0:T(1,128)}, u32[]{:S(2)}) copy-start(s32[1,6]{1,0:T(1,128)} %counts_ref.3) | copy-start | bytes 76
  34.2 7.0 %copy-start.2 = (bf16[1,32,3072]{2,1,0:T(8,128)(2,1)S(1)}, bf16[1,32,3072]{2,1,0:T(8,128)(2,1)}, u32[]{:S(2)}) copy-start(bf16[1,32,3072]{2,1,0:T(8,128)(2,1)} %param.9) | copy-start | bytes 589828
  34.3 9.8 %collective-permute-start.10 = (bf16[32,3072]{1,0:T(8,128)(2,1)S(1)}, bf16[32,3072]{1,0:T(8,128)(2,1)S(1)}, u32[]{:S(2)}, u32[]{:S(2)}) collective-permute-start(bf16[32,3072]{1,0:T(8,128)(2,1)S(1)} %get-tuple-element.113), channel_id=1, source_target_pairs={{0,3},{1,2},{2,1},{3,0},{4,7},{5,6},{6,5},{7,4},{8,11},{9,10},{10,... | collective-permute-start | bytes 589832 | tf_op jit(solution)/shard_map/ppermute | solution.py:447
  35.8 9.0 %collective-permute-start.11 = (bf16[32,3072]{1,0:T(8,128)(2,1)S(1)}, bf16[32,3072]{1,0:T(8,128)(2,1)S(1)}, u32[]{:S(2)}, u32[]{:S(2)}) collective-permute-start(bf16[32,3072]{1,0:T(8,128)(2,1)S(1)} %get-tuple-element.114), channel_id=1, source_target_pairs={{0,1},{1,0},{2,3},{3,2},{4,5},{5,4},{6,7},{7,6},{8,9},{9,8},{10,11... | collective-permute-start | bytes 589832 | tf_op jit(solution)/shard_map/ppermute | solution.py:447
  36.3 8.5 %collective-permute-start.12 = (bf16[32,3072]{1,0:T(8,128)(2,1)S(1)}, bf16[32,3072]{1,0:T(8,128)(2,1)S(1)}, u32[]{:S(2)}, u32[]{:S(2)}) collective-permute-start(bf16[32,3072]{1,0:T(8,128)(2,1)S(1)} %get-tuple-element.115), channel_id=1, source_target_pairs={{0,2},{1,3},{2,0},{3,1},{4,6},{5,7},{6,4},{7,5},{8,10},{9,11},{10,... | collective-permute-start | bytes 589832 | tf_op jit(solution)/shard_map/ppermute | solution.py:447
  41.3 7.5 %collective-permute-start.7 = (bf16[32,3072]{1,0:T(8,128)(2,1)S(1)}, bf16[32,3072]{1,0:T(8,128)(2,1)S(1)}, u32[]{:S(2)}, u32[]{:S(2)}) collective-permute-start(bf16[32,3072]{1,0:T(8,128)(2,1)S(1)} %bitcast.24), channel_id=1, source_target_pairs={{0,8},{1,9},{2,10},{3,11},{4,12},{5,13},{6,14},{7,15},{8,16},{9,17... | collective-permute-start | bytes 589832 | tf_op jit(solution)/shard_map/ppermute | solution.py:455
  41.4 9.0 %collective-permute-start.8 = (bf16[32,3072]{1,0:T(8,128)(2,1)S(1)}, bf16[32,3072]{1,0:T(8,128)(2,1)S(1)}, u32[]{:S(2)}, u32[]{:S(2)}) collective-permute-start(bf16[32,3072]{1,0:T(8,128)(2,1)S(1)} %get-tuple-element.110), channel_id=1, source_target_pairs={{0,11},{1,10},{2,9},{3,8},{4,15},{5,14},{6,13},{7,12},{8,19},{9,18... | collective-permute-start | bytes 589832 | tf_op jit(solution)/shard_map/ppermute | solution.py:455
  44.1 9.2 %collective-permute-start.9 = (bf16[32,3072]{1,0:T(8,128)(2,1)S(1)}, bf16[32,3072]{1,0:T(8,128)(2,1)S(1)}, u32[]{:S(2)}, u32[]{:S(2)}) collective-permute-start(bf16[32,3072]{1,0:T(8,128)(2,1)S(1)} %get-tuple-element.111), channel_id=1, source_target_pairs={{0,9},{1,8},{2,11},{3,10},{4,13},{5,12},{6,15},{7,14},{8,17},{9,16... | collective-permute-start | bytes 589832 | tf_op jit(solution)/shard_map/ppermute | solution.py:455
  45.0 13.4 %collective-permute-start.13 = (bf16[32,3072]{1,0:T(8,128)(2,1)S(1)}, bf16[32,3072]{1,0:T(8,128)(2,1)S(1)}, u32[]{:S(2)}, u32[]{:S(2)}) collective-permute-start(bf16[32,3072]{1,0:T(8,128)(2,1)S(1)} %add_terms.1), channel_id=1, source_target_pairs={{0,12},{1,13},{2,14},{3,15},{4,8},{5,9},{6,10},{7,11},{8,20},{9,21... | collective-permute-start | bytes 589832 | tf_op jit(solution)/shard_map/ppermute | solution.py:455
  46.9 11.4 %collective-permute-start.14 = (bf16[32,3072]{1,0:T(8,128)(2,1)S(1)}, bf16[32,3072]{1,0:T(8,128)(2,1)S(1)}, u32[]{:S(2)}, u32[]{:S(2)}) collective-permute-start(bf16[32,3072]{1,0:T(8,128)(2,1)S(1)} %get-tuple-element.119), channel_id=1, source_target_pairs={{0,10},{1,11},{2,8},{3,9},{4,14},{5,15},{6,12},{7,13},{8,18},{9,19... | collective-permute-start | bytes 589832 | tf_op jit(solution)/shard_map/ppermute | solution.py:455
  48.7 9.6 %collective-permute-start.15 = (bf16[32,3072]{1,0:T(8,128)(2,1)S(1)}, bf16[32,3072]{1,0:T(8,128)(2,1)S(1)}, u32[]{:S(2)}, u32[]{:S(2)}) collective-permute-start(bf16[32,3072]{1,0:T(8,128)(2,1)S(1)} %get-tuple-element.120), channel_id=1, source_target_pairs={{0,8},{1,9},{2,10},{3,11},{4,12},{5,13},{6,14},{7,15},{8,16},{9,17... | collective-permute-start | bytes 589832 | tf_op jit(solution)/shard_map/ppermute | solution.py:455
